TPU v7x, 512 devices: a whole 4x8x8 slice. The times are simulated.
512 devices in a mesh: snd: 64 (over y, z), rcv: 8 (over x, core).
Axes of the slice: x: 4, y: 8, z: 8, core: 2. Of those that a mesh axis runs over, the one named last changes fastest.
Arguments:
- tile_counts: bfloat16 [64, 8, 32, 256, 256], P('snd', 'rcv'), may hold values from 0 to 10, as said below
- tile_sender: int32 [64, 8, 32], P('snd', 'rcv'), may hold values from 0 to 3
- tile_receiver: int32 [64, 8, 32], P('snd', 'rcv'), may hold values from 0 to 31
- tile_action: int32 [64, 8, 32], P('snd', 'rcv'), may hold values from 0 to 255
- tile_fill: int32 [64, 8], P('snd', 'rcv'), may hold values from 1 to 32, as said below
- sender_log_shape: float32 [64, 96, 1024], P('snd', None, 'rcv'), may hold values from -0.5 to 3
- sender_log_rate: float32 [64, 96, 1024], P('snd', None, 'rcv')
- receiver_log_shape: float32 [8, 96, 8192], P('rcv', None, 'snd'), may hold values from -0.5 to 3
- receiver_log_rate: float32 [8, 96, 8192], P('rcv', None, 'snd')
- action_log_shape: float32 [96, 256], replicated, may hold values from -0.5 to 3
- action_log_rate: float32 [96, 256], replicated
Outputs:
- new_sender_log_shape: float32 [64, 96, 1024], P('snd', None, 'rcv')
- new_sender_log_rate: float32 [64, 96, 1024], P('snd', None, 'rcv')
- new_receiver_log_shape: float32 [8, 96, 8192], P('rcv', None, 'snd')
- new_receiver_log_rate: float32 [8, 96, 8192], P('rcv', None, 'snd')
- new_action_log_shape: float32 [96, 256], replicated
- new_action_log_rate: float32 [96, 256], replicated
Inputs may be any that keep to these rules, and one draw needn't show every extreme that they name: tile_fill[p, q] is the number of live slots of that device, its first slots; slots beyond it are ignored. In every draw some device has all 32 slots live. `tile_counts`: non-negative weighted counts; many entries are zero.
All inputs are finite; a program needn't handle non-finite values.
Results may differ from a plain program's by a relative error of at most 0.004.
Values may be sent and summed in bfloat16 or wider, within the bound.
A program may use at most 64 MiB of HBM per device.

v0:
```python
import jax
import jax.numpy as jnp
from jax import lax
from jax.sharding import PartitionSpec as P

prior_shape = 0.3
prior_rate = 0.3
step_size = 0.5
tile_group = 4


def digamma_series(value):
    shift_sum = jnp.zeros_like(value)
    for offset in range(6):
        shift_sum = shift_sum + 1.0 / (value + float(offset))
    moved = value + 6.0
    inverse = 1.0 / moved
    inv_square = inverse * inverse
    series = (
        jnp.log(moved)
        - 0.5 * inverse
        - inv_square * (1.0 / 12.0 - inv_square * (1.0 / 120.0 - inv_square / 252.0))
    )
    return series - shift_sum


def geometric(log_shape, log_rate):
    return jnp.exp(digamma_series(jnp.exp(log_shape)) - log_rate)


def refresh(log_value, target):
    return jnp.log((1.0 - step_size) * jnp.exp(log_value) + step_size * target)


def add_columns(running, addend, start_col):
    span_cols = addend.shape[1]
    current = lax.dynamic_slice_in_dim(running, start_col, span_cols, 1)
    return lax.dynamic_update_slice_in_dim(running, current + addend, start_col, 1)


def per_device(
    tile_counts,
    tile_sender,
    tile_receiver,
    tile_action,
    tile_fill,
    sender_log_shape,
    sender_log_rate,
    receiver_log_shape,
    receiver_log_rate,
    action_log_shape,
    action_log_rate,
):
    counts = tile_counts[0, 0]
    senders = tile_sender[0, 0]
    receivers = tile_receiver[0, 0]
    actions = tile_action[0, 0]
    live_count = tile_fill[0, 0]
    tile_edge = counts.shape[1]
    own_send_shape = sender_log_shape[0]
    own_send_rate = sender_log_rate[0]
    own_recv_shape = receiver_log_shape[0]
    own_recv_rate = receiver_log_rate[0]
    group_shape, group_rate = (
        lax.all_gather(own_send_shape, "rcv", axis=1, tiled=True),
        lax.all_gather(own_send_rate, "rcv", axis=1, tiled=True),
    )
    sender_geo = geometric(group_shape, group_rate).astype(jnp.bfloat16)
    group_shape, group_rate = (
        lax.all_gather(own_recv_shape, "snd", axis=1, tiled=True),
        lax.all_gather(own_recv_rate, "snd", axis=1, tiled=True),
    )
    receiver_geo = geometric(group_shape, group_rate).astype(jnp.bfloat16)
    sender_part = jnp.sum(jnp.exp(own_send_shape - own_send_rate), axis=1)
    receiver_part = jnp.sum(jnp.exp(own_recv_shape - own_recv_rate), axis=1)
    sender_total, receiver_total = lax.psum((sender_part, receiver_part), ("snd", "rcv"))
    action_geo = geometric(action_log_shape, action_log_rate)
    factor_rank = action_geo.shape[0]

    def one_turn(turn_index, totals):
        send_term, recv_term, act_term = totals
        first_slot = turn_index * tile_group
        slot_ids = first_slot + jnp.arange(tile_group, dtype=jnp.int32)
        live_flags = (slot_ids < live_count).astype(jnp.float32)
        block_counts = lax.dynamic_slice_in_dim(counts, first_slot, tile_group, 0)
        send_starts = [senders[first_slot + offset] * tile_edge for offset in range(tile_group)]
        recv_starts = [receivers[first_slot + offset] * tile_edge for offset in range(tile_group)]
        action_ids = [actions[first_slot + offset] for offset in range(tile_group)]
        send_blocks = jnp.stack(
            [
                lax.dynamic_slice_in_dim(sender_geo, start_col, tile_edge, 1)
                for start_col in send_starts
            ]
        )
        recv_blocks = jnp.stack(
            [
                lax.dynamic_slice_in_dim(receiver_geo, start_col, tile_edge, 1)
                for start_col in recv_starts
            ]
        )
        weights = jnp.stack(
            [lax.dynamic_slice_in_dim(action_geo, action_id, 1, 1) for action_id in action_ids]
        )
        scaled = (send_blocks.astype(jnp.float32) * weights).astype(jnp.bfloat16)
        expected = jnp.einsum(
            "tki,tkj->tij", scaled, recv_blocks, preferred_element_type=jnp.float32
        )
        ratios = (block_counts.astype(jnp.float32) * live_flags[:, None, None] / expected).astype(
            jnp.bfloat16
        )
        toward_send = jnp.einsum(
            "tkj,tij->tki", recv_blocks, ratios, preferred_element_type=jnp.float32
        )
        toward_recv = jnp.einsum("tki,tij->tkj", scaled, ratios, preferred_element_type=jnp.float32)
        send_part = scaled.astype(jnp.float32) * toward_send
        recv_part = recv_blocks.astype(jnp.float32) * toward_recv
        act_part = jnp.sum(send_part, axis=2)
        for offset in range(tile_group):
            send_term = add_columns(send_term, send_part[offset], send_starts[offset])
            recv_term = add_columns(recv_term, recv_part[offset], recv_starts[offset])
            act_term = add_columns(act_term, act_part[offset][:, None], action_ids[offset])
        return (send_term, recv_term, act_term)

    turns_needed = (live_count + tile_group - 1) // tile_group
    initial = (
        jnp.zeros((factor_rank, sender_geo.shape[1]), jnp.float32),
        jnp.zeros((factor_rank, receiver_geo.shape[1]), jnp.float32),
        jnp.zeros((factor_rank, action_geo.shape[1]), jnp.float32),
    )
    send_term, recv_term, act_term = lax.fori_loop(0, turns_needed, one_turn, initial)
    sender_stat = lax.psum_scatter(
        send_term.astype(jnp.bfloat16), "rcv", scatter_dimension=1, tiled=True
    ).astype(jnp.float32)
    receiver_stat = lax.psum_scatter(recv_term, "snd", scatter_dimension=1, tiled=True)
    action_stat = lax.psum(act_term, ("snd", "rcv"))
    action_total = jnp.sum(jnp.exp(action_log_shape - action_log_rate), axis=1)
    new_send_shape = refresh(own_send_shape, prior_shape + sender_stat)
    new_send_rate = refresh(own_send_rate, (prior_rate + receiver_total * action_total)[:, None])
    new_recv_shape = refresh(own_recv_shape, prior_shape + receiver_stat)
    new_recv_rate = refresh(own_recv_rate, (prior_rate + sender_total * action_total)[:, None])
    new_act_shape = refresh(action_log_shape, prior_shape + action_stat)
    new_act_rate = refresh(action_log_rate, (prior_rate + sender_total * receiver_total)[:, None])
    return (
        new_send_shape[None],
        new_send_rate[None],
        new_recv_shape[None],
        new_recv_rate[None],
        new_act_shape,
        new_act_rate,
    )


def solution(mesh):
    return jax.shard_map(
        per_device,
        mesh=mesh,
        in_specs=(
            P("snd", "rcv", None, None, None),
            P("snd", "rcv", None),
            P("snd", "rcv", None),
            P("snd", "rcv", None),
            P("snd", "rcv"),
            P("snd", None, "rcv"),
            P("snd", None, "rcv"),
            P("rcv", None, "snd"),
            P("rcv", None, "snd"),
            P(),
            P(),
        ),
        out_specs=(
            P("snd", None, "rcv"),
            P("snd", None, "rcv"),
            P("rcv", None, "snd"),
            P("rcv", None, "snd"),
            P(),
            P(),
        ),
        check_vma=False,
    )
```

profile of v0, /device:TPU:1, one launch (start us, length us, event | category | flops | bytes accessed | tf_op | source)
XLA Modules:
  0.0 1040.8 jit_solution(684271220119446146)
XLA Ops:
  11.3 106.9 %all-reduce = (f32[96]{0:T(128)S(1)}, f32[96]{0:T(128)S(1)}) all-reduce(f32[96]{0:T(128)S(1)} %exponential_reduce_fusion.2, f32[96]{0:T(128)S(1)} %exponential_reduce_fusion.1), channel_id=1, replica_groups=mesh['snd'=64,'rcv'=8] {'snd','rcv'}, use_global_device_ids=true, to_apply=%region_5.6 | all-reduce | flops 192 | bytes 1536 | tf_op jit(solution)/shard_map/psum | solution.py:76
  118.7 2.4 exponential_reduce_fusion
  121.9 14.2 %all-gather = f32[1,96,1024]{2,1,0:T(8,128)S(1)} all-gather(f32[1,96,128]{2,1,0:T(8,128)} %param.18), channel_id=2, replica_groups=mesh['snd'=64,'rcv'=8] {'rcv'}, dimensions={2}, use_global_device_ids=true | all-gather | bytes 442368 | tf_op jit(solution)/shard_map/all_gather | solution.py:65
  136.1 13.2 %all-gather.1 = f32[1,96,1024]{2,1,0:T(8,128)S(1)} all-gather(f32[1,96,128]{2,1,0:T(8,128)} %param.19), channel_id=3, replica_groups=mesh['snd'=64,'rcv'=8] {'rcv'}, dimensions={2}, use_global_device_ids=true | all-gather | bytes 442368 | tf_op jit(solution)/shard_map/all_gather | solution.py:66
  150.5 36.4 %all-gather.9.cloned.1.call-done = f32[1,96,8192]{2,1,0:T(8,128)} async-done(((f32[1,96,128]{2,1,0:T(8,128)}), f32[1,96,8192]{2,1,0:T(8,128)}) %all-gather.9.cloned.1.call-update) | async-done | bytes 3145744 | tf_op jit(solution)/shard_map/all_gather | solution.py:71
  186.9 7.1 fusion.26
  194.9 299.6 %while.16 = (s32[]{:T(128)}, f32[96,1024]{1,0:T(8,128)S(1)}, f32[96,8192]{1,0:T(8,128)S(1)}, f32[96,256]{0,1:T(8,128)}, s32[]{:T(128)}, /*index=5*/s32[32]{0:T(1...) while((s32[]{:T(128)}, f32[96,1024]{1,0:T(8,128)S(1)}, ...), condition=%wide.region_2.0_spmd, body=%wide.region_0.2_spmd.sunk | while | flops 155387072 | bytes 7230145 | solution.py:130
  212.4 1.5 fusion.72
  249.8 1.5 fusion.72
  287.3 1.5 fusion.72
  294.6 1.3 dynamic_update_slice.99
  324.8 1.5 fusion.72
  362.2 1.5 fusion.72
  374.5 1.3 dynamic_update_slice.101
  399.8 1.5 fusion.72
  437.2 1.5 fusion.72
  474.5 1.5 fusion.72
  494.6 1.9 copy.20
  497.2 1.8 copy.21
  501.1 255.9 %all-reduce.3.cloned.1.call-done = f32[96,256]{1,0:T(8,128)} async-done(((f32[96,256]{1,0:T(8,128)}), f32[96,256]{1,0:T(8,128)}) %all-reduce.3.cloned.1.call-update) | async-done | bytes 98320 | tf_op jit(solution)/shard_map/psum | solution.py:135
  757.0 1.6 multiply_log_fusion
  758.5 28.3 %reduce-scatter.7.cloned.1.call-done = bf16[128,96]{1,0:T(8,128)(2,1)} async-done(((bf16[1024,96]{1,0:T(8,128)(2,1)}), bf16[128,96]{1,0:T(8,128)(2,1)}) %reduce-scatter.7.cloned.1.call-update) | async-done | bytes 24592
  788.4 244.4 %reduce-scatter.5.cloned.1.call-done = f32[96,128]{1,0:T(8,128)} async-done(((f32[96,8192]{1,0:T(8,128)}), f32[96,128]{1,0:T(8,128)}) %reduce-scatter.5.cloned.1.call-update) | async-done | bytes 49168 | tf_op jit(solution)/shard_map/reduce_scatter | solution.py:134
  1032.8 1.4 fusion.37
  (251 shorter events, 197.1 us)
Async XLA Ops:
  7.2 143.3 %all-gather.7.cloned.1.call-start = ((), (), s32[]{:S(2)}) async-start(), calls=%async_computation.4 | async-start | bytes 3194880 | tf_op jit(solution)/shard_map/all_gather | solution.py:70
  7.9 179.0 %all-gather.9.cloned.1.call-start = ((), (), s32[]{:S(2)}) async-start(), calls=%async_computation.5 | async-start | bytes 3194880 | tf_op jit(solution)/shard_map/all_gather | solution.py:71
  8.7 748.3 %all-reduce.3.cloned.1.call-start = ((), (), s32[]{:S(2)}) async-start(), calls=%async_computation.3 | async-start | bytes 196608 | tf_op jit(solution)/shard_map/psum | solution.py:135
  118.1 0.6 copy-start.10
  118.1 0.6 copy-start.12
  193.9 1.0 copy-start.6
  193.9 1.0 copy-start.7
  193.9 1.0 copy-start.8
  494.5 4.6 copy-start
  494.5 5.1 copy-start.9
  494.5 5.1 copy-start.11
  494.5 5.1 copy-start.13
  496.5 290.4 %reduce-scatter.7.cloned.1.call-start = ((), (), s32[]{:S(2)}) async-start(), calls=%async_computation.6 | async-start | bytes 294912
  497.2 2.5 copy-start.1
  497.2 3.2 copy-start.2
  497.2 259.8 %copy-start.5 = (f32[96,256]{1,0:T(8,128)S(1)}, f32[96,256]{1,0:T(8,128)}, u32[]{:S(2)}) copy-start(f32[96,256]{1,0:T(8,128)} %param.22) | copy-start | bytes 294916
  497.2 290.5 %copy-start.3 = (f32[1,96,128]{2,1,0:T(8,128)S(1)}, f32[1,96,128]{2,1,0:T(8,128)}, u32[]{:S(2)}) copy-start(f32[1,96,128]{2,1,0:T(8,128)} %param.18) | copy-start | bytes 147460
  497.2 535.6 %copy-start.4 = (f32[1,96,128]{2,1,0:T(8,128)S(1)}, f32[1,96,128]{2,1,0:T(8,128)}, u32[]{:S(2)}) copy-start(f32[1,96,128]{2,1,0:T(8,128)} %param.20) | copy-start | bytes 147460
  499.0 533.8 %reduce-scatter.5.cloned.1.call-start = ((), (), s32[]{:S(2)}) async-start(), calls=%async_computation.2 | async-start | bytes 3194880 | tf_op jit(solution)/shard_map/reduce_scatter | solution.py:134
Sparse Core Ops, SparseCore 0:
  11.0 89.3 all-gather.6
  103.3 83.4 all-gather.8
  496.6 260.3 all-reduce.2
  759.8 26.9 reduce-scatter.6
  790.8 241.9 reduce-scatter.4
where the time goes:
time: 1050 us; the launch traced here: 1040 us
  waiting for transfers between devices  567 us (54%)
  blocking collectives  134 us (13%)
  other arithmetic  114 us (11%)
  loops' own time  98.8 us (9%)
  local copies, waits for them, and re-layouts  83.5 us (8%)
  matrix products  28.9 us (3%)
  between operations  14.6 us (1%)
    psum x1, waiting for transfers between devices, per_device(): action_stat = lax.psum(act_term, ('snd', 'rcv'))  256 us
    reduce_scatter x1, waiting for transfers between devices, per_device(): lax.psum_scatter(recv_term, 'snd', scatter_dimension=1, tiled=True)  244 us
    psum x1, blocking collectives, per_device(): lax.psum((sender_part, receiver_part), ('snd', 'rcv'))  107 us
    another operation x1, loops' own time, per_device(): lax.fori_loop(0, turns_needed, one_turn, initial)  98.8 us
    dynamic_update_slice x56, other arithmetic, add_columns(): lax.dynamic_update_slice_in_dim(running, current + addend, start_col, 1)  51.9 us
    dynamic_update_slice x32, local copies, waits for them, and re-layouts, add_columns(): lax.dynamic_update_slice_in_dim(running, current + addend, start_col, 1)  40.9 us
    add x32, other arithmetic, add_columns(): current + addend  38.1 us
    all_gather x1, waiting for transfers between devices, per_device(): lax.all_gather(own_recv_rate, 'snd', axis=1, tiled=True)  36.4 us
  transfers between devices with their start and end apart: 5, of which 4 were waited for; matrix products, arithmetic and copies ran while one was open for 1% of the time, Pallas kernels for 0%

commit v1 on v0

v1 whole, which is shorter than its diff:
```python
import functools

import jax
import jax.numpy as jnp
from jax import lax
from jax.experimental import pallas as pl
from jax.experimental.pallas import tpu as pltpu
from jax.sharding import PartitionSpec as P

prior_shape = 0.3
prior_rate = 0.3
step_size = 0.5
lanes = 128
unroll = 4

MESH = pl.DeviceIdType.MESH
bf16 = jnp.bfloat16
f32 = jnp.float32


def digamma_series(value):
    shift_sum = jnp.zeros_like(value)
    for offset in range(6):
        shift_sum = shift_sum + 1.0 / (value + float(offset))
    moved = value + 6.0
    inverse = 1.0 / moved
    inv_square = inverse * inverse
    series = (
        jnp.log(moved)
        - 0.5 * inverse
        - inv_square * (1.0 / 12.0 - inv_square * (1.0 / 120.0 - inv_square / 252.0))
    )
    return series - shift_sum


def geometric(log_shape, log_rate):
    return jnp.exp(digamma_series(jnp.exp(log_shape)) - log_rate)


def refresh(log_value, target):
    return jnp.log((1.0 - step_size) * jnp.exp(log_value) + step_size * target)


def turned(value):
    rank, cols = value.shape
    padded = jnp.concatenate([value, jnp.zeros((lanes - rank, cols), value.dtype)], axis=0)
    return padded.T


def place(side):
    snd = lax.axis_index("snd")
    return snd // side, lax.rem(snd, side), lax.axis_index("rcv")


def peer_y(y, z, side, offset):
    return {"snd": lax.rem(y + offset + side, side) * side + z}


def peer_z(y, z, side, offset):
    return {"snd": y * side + lax.rem(z + offset + side, side)}


def peer_r(rcv, n_rcv, offset):
    return {"rcv": lax.rem(rcv + offset, n_rcv)}


def greet(side, n_rcv):
    y, z, rcv = place(side)
    barrier = pltpu.get_barrier_semaphore()
    for offset in range(1, side):
        for peer in (peer_y, peer_z):
            pl.semaphore_signal(
                barrier, inc=1, device_id=peer(y, z, side, offset), device_id_type=MESH
            )
    for offset in range(1, n_rcv):
        pl.semaphore_signal(
            barrier, inc=1, device_id=peer_r(rcv, n_rcv, offset), device_id_type=MESH
        )
    return barrier, 2 * (side - 1) + n_rcv - 1


def send(src, dst, send_sem, recv_sem, device):
    copy = pltpu.make_async_remote_copy(
        src_ref=src,
        dst_ref=dst,
        send_sem=send_sem,
        recv_sem=recv_sem,
        device_id=device,
        device_id_type=MESH,
    )
    copy.start()
    return copy


def gather_kernel(
    side,
    n_rcv,
    rs_ref,
    rr_ref,
    ss_ref,
    sr_ref,
    as_ref,
    ar_ref,
    top_ref,
    low_ref,
    sgeo_ref,
    ageo_ref,
    tot_ref,
    near_send,
    near_recv,
    ring_send,
    ring_recv,
    rcv_send,
    rcv_recv,
):
    y, z, rcv = place(side)
    half = side // 2
    barrier, expected = greet(side, n_rcv)
    geo = geometric(rs_ref[0], rr_ref[0]).astype(bf16)
    rows = geo.shape[0] // 2
    top_ref[y, z] = geo[:rows]
    low_ref[z, y] = geo[rows:]
    pl.semaphore_wait(barrier, expected)

    near = []
    for offset in range(1, side):
        for kind in (0, 1):
            ref = (top_ref.at[y, z], low_ref.at[z, y])[kind]
            device = (peer_z, peer_y)[kind](y, z, side, offset)
            near.append(
                send(ref, ref, near_send.at[kind, offset], near_recv.at[kind, offset], device)
            )

    sgeo_ref[rcv] = turned(geometric(ss_ref[0], sr_ref[0])).astype(bf16)
    own = sgeo_ref.at[rcv]
    across = [
        send(own, own, rcv_send.at[o], rcv_recv.at[o], peer_r(rcv, n_rcv, o))
        for o in range(1, n_rcv)
    ]
    send_row = jnp.sum(turned(jnp.exp(ss_ref[0] - sr_ref[0])), axis=0, keepdims=True)
    recv_row = jnp.sum(turned(jnp.exp(rs_ref[0] - rr_ref[0])), axis=0, keepdims=True)
    row_id = lax.broadcasted_iota(jnp.int32, (8, lanes), 0)
    tot_ref[...] = jnp.where(row_id == 0, send_row, jnp.where(row_id == 1, recv_row, 0.0))
    ageo_ref[...] = turned(geometric(as_ref[...], ar_ref[...]))

    for copy in near:
        copy.wait()

    passed = {}
    for step in range(half):
        for piece in (0, 1):
            for kind in (0, 1):
                ref = (top_ref, low_ref)[kind]
                place_id = (y, z)[kind]
                peer = (peer_y, peer_z)[kind]
                for way in (0, 1):
                    if step == half - 1 and piece != way:
                        continue
                    if step > 0:
                        passed[step - 1, piece, kind, way].wait_recv()
                    sign = 1 - 2 * way
                    block = lax.rem(place_id - sign * step + side, side)
                    part = ref.at[block, pl.ds(piece * half, half)]
                    passed[step, piece, kind, way] = send(
                        part,
                        part,
                        ring_send.at[step, piece, kind, way],
                        ring_recv.at[step, piece, kind, way],
                        peer(y, z, side, sign),
                    )
    for (step, piece, kind, way), copy in passed.items():
        forwarded = step < half - 2 or (step == half - 2 and piece == way)
        if not forwarded:
            copy.wait_recv()
        copy.wait_send()
    for copy in across:
        copy.wait()


def tile_kernel(
    side,
    send_id,
    recv_id,
    act_id,
    fill,
    counts_ref,
    top_ref,
    low_ref,
    sgeo_ref,
    ageo_ref,
    top_out,
    low_out,
    send_out,
    act_out,
    counts,
    send_acc,
    recv_acc,
    load_sem,
):
    slots, edge = counts.shape[0], counts.shape[1]
    groups = slots // unroll
    span = edge // lanes
    rows = top_ref.shape[2]

    def load(group):
        part = pl.ds(group * unroll, unroll)
        return pltpu.make_async_copy(
            counts_ref.at[0, 0, part], counts.at[part], load_sem.at[group]
        )

    for group in range(groups):
        load(group).start()
    send_acc[...] = jnp.zeros_like(send_acc)
    act_out[...] = jnp.zeros_like(act_out)

    def clear(block, carry):
        recv_acc[block] = jnp.zeros(recv_acc.shape[1:], f32)
        return carry

    lax.fori_loop(0, recv_acc.shape[0], clear, 0)
    live_count = fill[0]

    def one_tile(slot):
        b, c, a = send_id[slot], recv_id[slot], act_id[slot]
        live = (slot < live_count).astype(f32)
        first = c * span
        y, z = first // side, lax.rem(first, side)
        recv = jnp.concatenate(
            [
                jnp.concatenate([top_ref[y, z + e] for e in range(span)], axis=1),
                jnp.concatenate([low_ref[z + e, y] for e in range(span)], axis=1),
            ],
            axis=0,
        )
        rank = recv.shape[0]
        recv_pad = jnp.concatenate([recv, jnp.zeros((lanes - rank, edge), bf16)], axis=0)
        sender = sgeo_ref[pl.ds(b * span, span)].reshape(edge, lanes)
        scaled = (sender.astype(f32) * ageo_ref[pl.ds(a, 1), :]).astype(bf16)
        expected = jnp.dot(scaled, recv_pad, preferred_element_type=f32)
        ratios = (counts[slot].astype(f32) * live / expected).astype(bf16)
        toward_send = lax.dot_general(
            ratios, recv_pad, (((1,), (1,)), ((), ())), preferred_element_type=f32
        )
        toward_recv = lax.dot_general(
            scaled, ratios, (((0,), (0,)), ((), ())), preferred_element_type=f32
        )
        send_part = scaled.astype(f32) * toward_send
        recv_part = recv.astype(f32) * toward_recv[:rank]
        return b, c, a, send_part, recv_part, jnp.sum(send_part, axis=0, keepdims=True)

    def one_group(group, carry):
        load(group).wait()

        @pl.when(group * unroll < live_count)
        def _():
            done = [one_tile(group * unroll + u) for u in range(unroll)]
            for b, c, a, send_part, recv_part, act_part in done:
                send_acc[pl.ds(b * span, span)] += send_part.reshape(span, lanes, lanes)
                recv_acc[c] += recv_part
                act_out[pl.ds(a, 1), :] += act_part

        return carry

    lax.fori_loop(0, groups, one_group, 0)
    send_out[...] = send_acc[...].astype(bf16)

    def hand_over(block, carry):
        value = recv_acc[block].astype(bf16)
        first = block * span
        y, z = first // side, lax.rem(first, side)
        for e in range(span):
            top_out[y, z + e] = value[:rows, e * lanes : (e + 1) * lanes]
            low_out[z + e, y] = value[rows:, e * lanes : (e + 1) * lanes]
        return carry

    lax.fori_loop(0, recv_acc.shape[0], hand_over, 0)


def reduce_kernel(
    side,
    n_rcv,
    top_ref,
    low_ref,
    send_ref,
    act_ref,
    tot_ref,
    recv_out,
    send_out,
    act_out,
    tot_out,
    ring_src,
    ring_dst,
    near_src,
    near_dst,
    send_dst,
    act_own,
    act_dst,
    sum_src,
    sum_dst,
    ring_send,
    ring_recv,
    near_send,
    near_recv,
    rcv_send,
    rcv_recv,
    sum_send,
    sum_recv,
    back_send,
    back_recv,
):
    y, z, rcv = place(side)
    half = side // 2
    act_rows = act_out.shape[0] // n_rcv
    barrier, expected = greet(side, n_rcv)
    for chunk in range(n_rcv):
        act_own[chunk, :act_rows] = act_ref[pl.ds(chunk * act_rows, act_rows), :]
        act_own[chunk, act_rows:] = tot_ref[...]
    pl.semaphore_wait(barrier, expected)

    refs, where, peers = (top_ref, low_ref), (y, z), (peer_y, peer_z)
    cross = (peer_z, peer_y)
    ring = {}

    def start_ring(step, piece, kind, way, src):
        ring[step, piece, kind, way] = send(
            src,
            ring_dst.at[kind, way, step, piece],
            ring_send.at[step, piece, kind, way],
            ring_recv.at[step, piece, kind, way],
            peers[kind](y, z, side, 1 - 2 * way),
        )

    def block_of(step, kind, way):
        sign = 1 - 2 * way
        return lax.rem(where[kind] + sign * (half - step) + side, side)

    for kind in (0, 1):
        for way in (0, 1):
            for step, piece in ((0, way), (1, 1 - way)):
                part = refs[kind].at[block_of(step, kind, way), pl.ds(piece * half, half)]
                start_ring(step, piece, kind, way, part)

    act_copies, send_copies = [], []
    for o in range(1, n_rcv):
        other = lax.rem(rcv + o, n_rcv)
        act_copies.append(
            send(
                act_own.at[other],
                act_dst.at[rcv],
                rcv_send.at[0, o],
                rcv_recv.at[0, o],
                {"rcv": other},
            )
        )
    for o in range(1, n_rcv):
        other = lax.rem(rcv + o, n_rcv)
        send_copies.append(
            send(
                send_ref.at[other],
                send_dst.at[rcv],
                rcv_send.at[1, o],
                rcv_recv.at[1, o],
                {"rcv": other},
            )
        )
    act_dst[rcv] = act_own[rcv]
    send_dst[rcv] = send_ref[rcv]

    def total_of(ref, count):
        value = ref[0].astype(f32)
        for index in range(1, count):
            value = value + ref[index].astype(f32)
        return value

    def spread(level, value):
        me = where[level]
        sum_src[level] = value
        sum_dst[level, me] = value
        return [
            send(
                sum_src.at[level],
                sum_dst.at[level, me],
                sum_send.at[level, o],
                sum_recv.at[level, o],
                peers[level](y, z, side, o),
            )
            for o in range(1, side)
        ]

    sums = [None, None]
    for step in range(1, half):
        for piece in (0, 1):
            for kind in (0, 1):
                for way in (0, 1):
                    if step == 1 and piece != way:
                        continue
                    ring[step - 1, piece, kind, way].wait_recv()
                    part = refs[kind][block_of(step, kind, way), pl.ds(piece * half, half)]
                    came = ring_dst[kind, way, step - 1, piece]
                    ring_src[kind, way, step - 1, piece] = (
                        part.astype(f32) + came.astype(f32)
                    ).astype(bf16)
                    start_ring(step, piece, kind, way, ring_src.at[kind, way, step - 1, piece])
        if step == 1:
            for copy in act_copies:
                copy.wait()
            sums[0] = spread(0, total_of(act_dst, n_rcv))
        if step == 2:
            for copy in sums[0]:
                copy.wait()
            sums[1] = spread(1, total_of(sum_dst.at[0], side))
    if sums[1] is None:
        for copy in sums[0]:
            copy.wait()
        sums[1] = spread(1, total_of(sum_dst.at[0], side))

    near, held = [], []
    for kind in (0, 1):
        for piece in (0, 1):
            part = refs[kind][where[kind], pl.ds(piece * half, half)].astype(f32)
            for way in (0, 1):
                ring[half - 1, piece, kind, way].wait_recv()
                part = part + ring_dst[kind, way, half - 1, piece].astype(f32)
            near_src[kind, pl.ds(piece * half, half)] = part.astype(bf16)
        mine = where[1 - kind]
        for o in range(1, side):
            other = lax.rem(mine + o, side)
            near.append(
                send(
                    near_src.at[kind, other],
                    near_dst.at[kind, mine],
                    near_send.at[kind, o],
                    near_recv.at[kind, o],
                    cross[kind](y, z, side, o),
                )
            )
        near_dst[kind, mine] = near_src[kind, mine]

    for copy in sums[1]:
        copy.wait()
    full = total_of(sum_dst.at[1], side)
    act_out[pl.ds(rcv * act_rows, act_rows), :] = full[:act_rows]
    tot_out[...] = full[act_rows:]
    own = act_out.at[pl.ds(rcv * act_rows, act_rows), :]
    back = [
        send(own, own, back_send.at[o], back_recv.at[o], peer_r(rcv, n_rcv, o))
        for o in range(1, n_rcv)
    ]
    for copy in send_copies:
        copy.wait()
    send_out[...] = total_of(send_dst, n_rcv)
    for copy in near:
        copy.wait()
    rows = recv_out.shape[0] // 2
    for kind in (0, 1):
        recv_out[kind * rows : (kind + 1) * rows] = total_of(near_dst.at[kind], side)
    for copy in ring.values():
        copy.wait_send()
    for copy in back:
        copy.wait()


def refresh_kernel(
    ss_ref,
    sr_ref,
    rs_ref,
    rr_ref,
    as_ref,
    ar_ref,
    send_ref,
    recv_ref,
    act_ref,
    tot_ref,
    ss_out,
    sr_out,
    rs_out,
    rr_out,
    as_out,
    ar_out,
):
    rank = as_ref.shape[0]
    row = lax.broadcasted_iota(jnp.int32, (rank, lanes), 0)
    col = lax.broadcasted_iota(jnp.int32, (rank, lanes), 1)

    def column(index):
        wide = jnp.broadcast_to(tot_ref[pl.ds(index, 1), :], (rank, lanes))
        return jnp.sum(jnp.where(row == col, wide, 0.0), axis=1, keepdims=True)

    send_total, recv_total = column(0), column(1)
    act_total = jnp.sum(jnp.exp(as_ref[...] - ar_ref[...]), axis=1, keepdims=True)
    ss_out[0] = refresh(ss_ref[0], prior_shape + send_ref[...].T[:rank])
    sr_out[0] = refresh(sr_ref[0], prior_rate + recv_total * act_total)
    rs_out[0] = refresh(rs_ref[0], prior_shape + recv_ref[...])
    rr_out[0] = refresh(rr_ref[0], prior_rate + send_total * act_total)
    as_out[...] = refresh(as_ref[...], prior_shape + act_ref[...].T[:rank])
    ar_out[...] = refresh(ar_ref[...], prior_rate + send_total * recv_total)


def per_device(
    side,
    n_rcv,
    tile_counts,
    tile_sender,
    tile_receiver,
    tile_action,
    tile_fill,
    ss,
    sr,
    rs,
    rr,
    ash,
    art,
):
    rank, actions = ash.shape
    slots, edge = tile_counts.shape[2], tile_counts.shape[3]
    rows, half = rank // 2, side // 2
    vmem = pl.BlockSpec(memory_space=pltpu.VMEM)
    smem = pl.BlockSpec(memory_space=pltpu.SMEM)
    shape = jax.ShapeDtypeStruct
    dma = pltpu.SemaphoreType.DMA

    top, low, sgeo, ageo, tot = pl.pallas_call(
        functools.partial(gather_kernel, side, n_rcv),
        out_shape=(
            shape((side, side, rows, lanes), bf16),
            shape((side, side, rows, lanes), bf16),
            shape((n_rcv, lanes, lanes), bf16),
            shape((actions, lanes), f32),
            shape((8, lanes), f32),
        ),
        in_specs=[vmem] * 6,
        out_specs=(vmem,) * 5,
        scratch_shapes=[
            dma((2, side)),
            dma((2, side)),
            dma((half, 2, 2, 2)),
            dma((half, 2, 2, 2)),
            dma((n_rcv,)),
            dma((n_rcv,)),
        ],
        compiler_params=pltpu.CompilerParams(
            collective_id=0, has_side_effects=True, vmem_limit_bytes=16 << 20
        ),
    )(rs, rr, ss, sr, ash, art)

    blocks = side * side * lanes // edge
    top_part, low_part, send_part, act_part = pl.pallas_call(
        functools.partial(tile_kernel, side),
        out_shape=(
            shape((side, side, rows, lanes), bf16),
            shape((side, side, rows, lanes), bf16),
            shape((n_rcv, lanes, lanes), bf16),
            shape((actions, lanes), f32),
        ),
        in_specs=[smem] * 4 + [pl.BlockSpec(memory_space=pl.ANY)] + [vmem] * 4,
        out_specs=(vmem,) * 4,
        scratch_shapes=[
            pltpu.VMEM((slots, edge, edge), bf16),
            pltpu.VMEM((n_rcv, lanes, lanes), f32),
            pltpu.VMEM((blocks, rank, edge), f32),
            dma((slots // unroll,)),
        ],
        compiler_params=pltpu.CompilerParams(vmem_limit_bytes=32 << 20),
    )(
        tile_sender.reshape(slots),
        tile_receiver.reshape(slots),
        tile_action.reshape(slots),
        tile_fill.reshape(1),
        tile_counts,
        top,
        low,
        sgeo,
        ageo,
    )

    chunk = actions // n_rcv + 8
    recv_stat, send_stat, act_stat, totals = pl.pallas_call(
        functools.partial(reduce_kernel, side, n_rcv),
        out_shape=(
            shape((rank, lanes), f32),
            shape((lanes, lanes), f32),
            shape((actions, lanes), f32),
            shape((8, lanes), f32),
        ),
        in_specs=[vmem] * 5,
        out_specs=(vmem,) * 4,
        scratch_shapes=[
            pltpu.VMEM((2, 2, half - 1, 2, half, rows, lanes), bf16),
            pltpu.VMEM((2, 2, half, 2, half, rows, lanes), bf16),
            pltpu.VMEM((2, side, rows, lanes), bf16),
            pltpu.VMEM((2, side, rows, lanes), bf16),
            pltpu.VMEM((n_rcv, lanes, lanes), bf16),
            pltpu.VMEM((n_rcv, chunk, lanes), f32),
            pltpu.VMEM((n_rcv, chunk, lanes), f32),
            pltpu.VMEM((2, chunk, lanes), f32),
            pltpu.VMEM((2, side, chunk, lanes), f32),
            dma((half, 2, 2, 2)),
            dma((half, 2, 2, 2)),
            dma((2, side)),
            dma((2, side)),
            dma((2, n_rcv)),
            dma((2, n_rcv)),
            dma((2, side)),
            dma((2, side)),
            dma((n_rcv,)),
            dma((n_rcv,)),
        ],
        compiler_params=pltpu.CompilerParams(
            collective_id=1, has_side_effects=True, vmem_limit_bytes=24 << 20
        ),
    )(top_part, low_part, send_part, act_part, tot)

    return pl.pallas_call(
        refresh_kernel,
        out_shape=tuple(shape(x.shape, f32) for x in (ss, sr, rs, rr, ash, art)),
        in_specs=[vmem] * 10,
        out_specs=(vmem,) * 6,
        compiler_params=pltpu.CompilerParams(vmem_limit_bytes=16 << 20),
    )(ss, sr, rs, rr, ash, art, send_stat, recv_stat, act_stat, totals)


def solution(mesh):
    n_snd, n_rcv = mesh.shape["snd"], mesh.shape["rcv"]
    side = round(n_snd**0.5)
    return jax.shard_map(
        functools.partial(per_device, side, n_rcv),
        mesh=mesh,
        in_specs=(
            P("snd", "rcv", None, None, None),
            P("snd", "rcv", None),
            P("snd", "rcv", None),
            P("snd", "rcv", None),
            P("snd", "rcv"),
            P("snd", None, "rcv"),
            P("snd", None, "rcv"),
            P("rcv", None, "snd"),
            P("rcv", None, "snd"),
            P(),
            P(),
        ),
        out_specs=(
            P("snd", None, "rcv"),
            P("snd", None, "rcv"),
            P("rcv", None, "snd"),
            P("rcv", None, "snd"),
            P(),
            P(),
        ),
        check_vma=False,
    )
```

time: 1050 us -> 88 us (0.08)
  waiting for transfers between devices: 567 us -> 0 us
  blocking collectives: 134 us -> 0 us
  other arithmetic: 114 us -> 0 us
  loops' own time: 98.8 us -> 0 us
  Pallas kernels: 0 us -> 76.9 us
  local copies, waits for them, and re-layouts: 83.5 us -> 9.14 us
  matrix products: 28.9 us -> 0 us
  between operations: 14.6 us -> 1.4 us
    psum x1 -> x0, waiting for transfers between devices: 256 us -> none  [per_device(): action_stat = lax.psum(act_term, ('snd', 'rcv'))]
    reduce_scatter x1 -> x0, waiting for transfers between devices: 244 us -> none  [per_device(): lax.psum_scatter(recv_term, 'snd', scatter_dimension=1, tiled=True)]
    psum x1 -> x0, blocking collectives: 107 us -> none  [per_device(): lax.psum((sender_part, receiver_part), ('snd', 'rcv'))]
    another operation x1 -> x0, loops' own time: 98.8 us -> none  [per_device(): lax.fori_loop(0, turns_needed, one_turn, initial)]
    pallas_call x0 -> x4, Pallas kernels: none -> 76.9 us  [the longest x1 37.7 us: per_device(): pl.pallas_call(functools.partial(reduce_kernel, side, n_rcv), out_shape=(...]
    dynamic_update_slice x56 -> x0, other arithmetic: 51.9 us -> none  [add_columns(): lax.dynamic_update_slice_in_dim(running, current + addend, start_col, 1)]
    dynamic_update_slice x32 -> x0, local copies, waits for them, and re-layouts: 40.9 us -> none  [add_columns(): lax.dynamic_update_slice_in_dim(running, current + addend, start_col, 1)]
    add x32 -> x0, other arithmetic: 38.1 us -> none  [add_columns(): current + addend]
  transfers between devices with their start and end apart: 5 -> 0, of which waited for: 4 -> 0; matrix products, arithmetic and copies ran while one was open for 1% -> 0% of each run, Pallas kernels for 0% -> 0%
where the time goes in v1:
time: 88 us; the launch traced here: 87.5 us
  Pallas kernels  76.9 us (87%)
  local copies, waits for them, and re-layouts  9.14 us (10%)
  between operations  1.4 us (2%)
    pallas_call x1, Pallas kernels, per_device(): pl.pallas_call(functools.partial(reduce_kernel, side, n_rcv), out_shape=(...  37.7 us
    pallas_call x1, Pallas kernels, per_device(): pl.pallas_call(functools.partial(gather_kernel, side, n_rcv), out_shape=(...  32.9 us
    unnamed x32, local copies, waits for them, and re-layouts  9.14 us
    pallas_call x1, Pallas kernels, per_device(): pl.pallas_call(functools.partial(tile_kernel, side), out_shape=(shape((si...  5.52 us

profile of v1, /device:TPU:1, one launch (start us, length us, event | category | flops | bytes accessed | tf_op | source)
XLA Modules:
  0.0 87.5 jit_solution(15254770012142112866)
XLA Ops:
  1.3 0.0 copy-start.1
  1.3 0.9 %copy-done.1 = f32[96,256]{1,0:T(8,128)S(1)} copy-done((f32[96,256]{1,0:T(8,128)S(1)}, f32[96,256]{1,0:T(8,128)}, u32[]{:S(2)}) %copy-start.1) | copy-done | bytes 98328
  2.2 0.9 %copy-done.3 = f32[96,256]{1,0:T(8,128)S(1)} copy-done((f32[96,256]{1,0:T(8,128)S(1)}, f32[96,256]{1,0:T(8,128)}, u32[]{:S(2)}) %copy-start.3) | copy-done | bytes 98328
  3.1 0.8 copy-done.5
  3.9 0.8 copy-done.7
  4.7 0.8 copy-done.9
  5.5 0.8 copy-done.11
  6.3 0.0 copy-start.10
  6.3 0.0 copy-start.12
  6.3 32.9 %shard_map.154 = (bf16[8,8,48,128]{3,2,1,0:T(8,128)(2,1)S(1)}, bf16[8,8,48,128]{3,2,1,0:T(8,128)(2,1)S(1)}, bf16[8,128,128]{2,1,0:T(8,128)(2,1)S(1)}, f32[256,128]{1,0:T(8,128)S(1)}, f32[8,128]{1,0:T(8,128)S(1)}) custom-call(f32[1,96,128]{2,1,0:T(8,128)S(1)} %copy-done.9, f32[1,96,128]{2,1,0:T(8,128)S(1)} %copy-done.11, f32[1,96,128]{2,1,0:T(8,128)S(1)} %copy-done.5, ...), custom_call_target="tpu_custom_call" | custom-call | tf_op jit(solution)/shard_map/pallas_call | solution.py:522
  39.2 0.0 copy-start
  39.2 2.2 %copy-done = bf16[1,1,32,256,256]{4,3,2,1,0:T(8,128)(2,1)S(1)} copy-done((bf16[1,1,32,256,256]{4,3,2,1,0:T(8,128)(2,1)S(1)}, bf16[1,1,32,256,256]{4,3,2,1,0:T(8,128)(2,1)}, u32[]{:S(2)}) %copy-start) | copy-done | bytes 4194328
  41.4 0.7 copy-done.13
  42.0 0.7 copy-done.14
  42.7 0.7 copy-done.15
  43.4 5.5 %shard_map.155 = (bf16[8,8,48,128]{3,2,1,0:T(8,128)(2,1)S(1)}, bf16[8,8,48,128]{3,2,1,0:T(8,128)(2,1)S(1)}, bf16[8,128,128]{2,1,0:T(8,128)(2,1)S(1)}, f32[256,128]{1,0:T(8,128)S(1)}) custom-call(s32[32]{0:T(128)S(1)} %bitcast.5, s32[32]{0:T(128)S(1)} %bitcast.6, s32[32]{0:T(128)S(1)} %bitcast.7, s32[1]{0:T(128)} %bitcast.4.fill, ...), custom_call_target="tpu_custom_call" | custom-call | tf_op jit(solution)/shard_map/pallas_call | solution.py:547
  48.9 37.7 %shard_map.156 = (f32[96,128]{1,0:T(8,128)S(1)}, f32[128,128]{1,0:T(8,128)S(1)}, f32[256,128]{1,0:T(8,128)S(1)}, f32[8,128]{1,0:T(8,128)S(1)}) custom-call(bf16[8,8,48,128]{3,2,1,0:T(8,128)(2,1)S(1)} %get-tuple-element.23.top_ref, bf16[8,8,48,128]{3,2,1,0:T(8,128)(2,1)S(1)} %get-tuple-element.24.low_ref, ...), custom_call_target="tpu_custom_call" | custom-call | tf_op jit(solution)/shard_map/pallas_call | solution.py:577
  86.6 0.0 copy-done.2
  86.6 0.0 copy-done.4
  86.6 0.0 copy-done.6
  86.6 0.0 copy-done.8
  86.6 0.0 copy-done.10
  86.6 0.0 copy-done.12
  86.6 0.9 shard_map.157
  (12 shorter events, 0.0 us)
Async XLA Ops:
  1.3 0.9 %copy-start.1 = (f32[96,256]{1,0:T(8,128)S(1)}, f32[96,256]{1,0:T(8,128)}, u32[]{:S(2)}) copy-start(f32[96,256]{1,0:T(8,128)} %as_ref.3) | copy-start | bytes 294916
  2.2 0.9 %copy-start.3 = (f32[96,256]{1,0:T(8,128)S(1)}, f32[96,256]{1,0:T(8,128)}, u32[]{:S(2)}) copy-start(f32[96,256]{1,0:T(8,128)} %ar_ref.3) | copy-start | bytes 294916
  3.1 0.8 copy-start.5
  3.9 0.8 copy-start.7
  4.7 0.8 copy-start.9
  5.5 0.8 copy-start.11
  6.3 80.3 %copy-start.2 = (f32[96,256]{1,0:T(8,128)S(1)}, f32[96,256]{1,0:T(8,128)}, u32[]{:S(2)}) copy-start(f32[96,256]{1,0:T(8,128)} %as_ref.3) | copy-start | bytes 294916
  6.3 80.3 %copy-start.4 = (f32[96,256]{1,0:T(8,128)S(1)}, f32[96,256]{1,0:T(8,128)}, u32[]{:S(2)}) copy-start(f32[96,256]{1,0:T(8,128)} %ar_ref.3) | copy-start | bytes 294916
  6.3 80.3 %copy-start.6 = (f32[1,96,128]{2,1,0:T(8,128)S(1)}, f32[1,96,128]{2,1,0:T(8,128)}, u32[]{:S(2)}) copy-start(f32[1,96,128]{2,1,0:T(8,128)} %ss_ref.3) | copy-start | bytes 147460
  6.3 80.3 %copy-start.8 = (f32[1,96,128]{2,1,0:T(8,128)S(1)}, f32[1,96,128]{2,1,0:T(8,128)}, u32[]{:S(2)}) copy-start(f32[1,96,128]{2,1,0:T(8,128)} %sr_ref.3) | copy-start | bytes 147460
  6.3 80.3 %copy-start.10 = (f32[1,96,128]{2,1,0:T(8,128)S(1)}, f32[1,96,128]{2,1,0:T(8,128)}, u32[]{:S(2)}) copy-start(f32[1,96,128]{2,1,0:T(8,128)} %rs_ref.3) | copy-start | bytes 147460
  6.3 80.3 %copy-start.12 = (f32[1,96,128]{2,1,0:T(8,128)S(1)}, f32[1,96,128]{2,1,0:T(8,128)}, u32[]{:S(2)}) copy-start(f32[1,96,128]{2,1,0:T(8,128)} %rr_ref.3) | copy-start | bytes 147460
  39.2 2.2 %copy-start = (bf16[1,1,32,256,256]{4,3,2,1,0:T(8,128)(2,1)S(1)}, bf16[1,1,32,256,256]{4,3,2,1,0:T(8,128)(2,1)}, u32[]{:S(2)}) copy-start(bf16[1,1,32,256,256]{4,3,2,1,0:T(8,128)(2,1)} %counts_ref.1) | copy-start | bytes 12582916
  41.4 0.7 copy-start.13
  42.0 0.7 copy-start.14
  42.7 0.7 copy-start.15

commit v2 on v0

v2 whole, which is shorter than its diff:
```python
import functools

import jax
import jax.numpy as jnp
from jax import lax
from jax.experimental import pallas as pl
from jax.experimental.pallas import tpu as pltpu
from jax.sharding import PartitionSpec as P

prior_shape = 0.3
prior_rate = 0.3
step_size = 0.5
lanes = 128
unroll = 4
whole_vmem = 60 << 20

MESH = pl.DeviceIdType.MESH
bf16 = jnp.bfloat16
f32 = jnp.float32


def digamma_series(value):
    shift_sum = jnp.zeros_like(value)
    for offset in range(6):
        shift_sum = shift_sum + 1.0 / (value + float(offset))
    moved = value + 6.0
    inverse = 1.0 / moved
    inv_square = inverse * inverse
    series = (
        jnp.log(moved)
        - 0.5 * inverse
        - inv_square * (1.0 / 12.0 - inv_square * (1.0 / 120.0 - inv_square / 252.0))
    )
    return series - shift_sum


def geometric(log_shape, log_rate):
    return jnp.exp(digamma_series(jnp.exp(log_shape)) - log_rate)


def refresh(log_value, target):
    return jnp.log((1.0 - step_size) * jnp.exp(log_value) + step_size * target)


def turned(value):
    rank, cols = value.shape
    padded = jnp.concatenate([value, jnp.zeros((lanes - rank, cols), value.dtype)], axis=0)
    return padded.T


def place(side):
    snd = lax.axis_index("snd")
    return snd // side, lax.rem(snd, side), lax.axis_index("rcv")


def peer_y(y, z, side, offset):
    return {"snd": lax.rem(y + offset + side, side) * side + z}


def peer_z(y, z, side, offset):
    return {"snd": y * side + lax.rem(z + offset + side, side)}


def peer_r(rcv, n_rcv, offset):
    return {"rcv": lax.rem(rcv + offset, n_rcv)}


def greet(side, n_rcv):
    y, z, rcv = place(side)
    barrier = pltpu.get_barrier_semaphore()
    for offset in far_first(side):
        for peer in (peer_y, peer_z):
            pl.semaphore_signal(
                barrier, inc=1, device_id=peer(y, z, side, offset), device_id_type=MESH
            )
    for offset in range(1, n_rcv):
        pl.semaphore_signal(
            barrier, inc=1, device_id=peer_r(rcv, n_rcv, offset), device_id_type=MESH
        )
    return barrier, 2 * (side - 1) + n_rcv - 1


def far_first(side):
    return sorted(range(1, side), key=lambda o: -min(o, side - o))


def slot_of(offset, side):
    return 0 if offset == 0 else (2 * offset - 1 if offset <= side // 2 else 2 * (side - offset))


def slot_at(offset, side):
    offset = lax.rem(offset + side, side)
    near = jnp.maximum(2 * offset - 1, 0)
    return jnp.where(offset <= side // 2, near, 2 * (side - offset))


class Sender:
    def __init__(self, send_sem, recv_sem):
        self.send_sem, self.recv_sem, self.count, self.sent = send_sem, recv_sem, 0, []

    def __call__(self, src, dst, device):
        at = self.count
        self.count += 1
        copy = pltpu.make_async_remote_copy(
            src_ref=src,
            dst_ref=dst,
            send_sem=self.send_sem.at[at // 16, at % 16],
            recv_sem=self.recv_sem.at[at // 16, at % 16],
            device_id=device,
            device_id_type=MESH,
        )
        copy.start()
        self.sent.append(copy)
        return copy


def split3(value):
    high = value.astype(bf16).astype(f32)
    middle = (value - high).astype(bf16).astype(f32)
    return high, middle, value - high - middle


def fused_kernel(
    side,
    n_rcv,
    counts_hbm,
    sid_hbm,
    rid_hbm,
    aid_hbm,
    fill_hbm,
    ss_hbm,
    sr_hbm,
    rs_hbm,
    rr_hbm,
    as_hbm,
    ar_hbm,
    recv_out,
    send_out,
    act_out,
    tot_out,
    ss_ref,
    sr_ref,
    rs_ref,
    rr_ref,
    as_ref,
    ar_ref,
    sid,
    rid,
    aid,
    fill,
    aid_row,
    prev,
    last_recv,
    last_send,
    counts,
    top_ref,
    low_ref,
    sgeo_ref,
    ageo_ref,
    send_slots,
    recv_slots,
    act_rows,
    parts,
    from1,
    from2,
    from3,
    from4,
    joined,
    near_src,
    near_dst,
    send_part,
    send_dst,
    act_own,
    act_dst,
    sum_src,
    sum_dst,
    load_sem,
    count_sem,
    send_sem,
    recv_sem,
):
    y, z, rcv = place(side)
    half = side // 2
    slots, edge = counts.shape[0], counts.shape[1]
    span = edge // lanes
    rank, rows = rs_ref.shape[1], top_ref.shape[2]
    actions = ageo_ref.shape[0]
    blocks, send_blocks = side * side // span, n_rcv // span

    loads = [
        pltpu.make_async_copy(src, dst, load_sem.at[index])
        for index, (src, dst) in enumerate(
            (
                (rs_hbm, rs_ref),
                (rr_hbm, rr_ref),
                (ss_hbm, ss_ref),
                (sr_hbm, sr_ref),
                (as_hbm, as_ref),
                (ar_hbm, ar_ref),
                (sid_hbm, sid),
                (rid_hbm, rid),
                (aid_hbm, aid),
                (fill_hbm, fill),
                (aid_hbm, aid_row),
            )
        )
    ]
    for copy in loads:
        copy.start()
    barrier, greeted = greet(side, n_rcv)
    count_loads = [
        pltpu.make_async_copy(
            counts_hbm.at[0, 0, pl.ds(group * unroll, unroll)],
            counts.at[pl.ds(group * unroll, unroll)],
            count_sem.at[group],
        )
        for group in range(slots // unroll)
    ]
    for copy in count_loads:
        copy.start()
    for copy in loads[:4]:
        copy.wait()
    geo = geometric(rs_ref[0], rr_ref[0]).astype(bf16)
    top_ref[y, 0] = geo[:rows]
    low_ref[z, 0] = geo[rows:]
    sgeo_ref[rcv] = turned(geometric(ss_ref[0], sr_ref[0])).astype(bf16)
    go = Sender(send_sem, recv_sem)
    pl.semaphore_wait(barrier, greeted)

    refs, where = (top_ref, low_ref), (y, z)
    ring_peer, near_peer = (peer_y, peer_z), (peer_z, peer_y)
    pieces = [(at, side // 4) for at in range(0, side, side // 4)]
    near, first, second = {}, {}, []

    def to_ring(kind, distance):
        return ring_peer[kind](y, z, side, distance)

    def step_one(start, size):
        for kind in (0, 1):
            for slot in range(max(start, 1), start + size):
                near[kind, slot].wait_recv()
            part = refs[kind].at[where[kind], pl.ds(start, size)]
            for distance in (2, -2, 1, -1):
                first[kind, start, distance] = go(part, part, to_ring(kind, distance))

    def step_two(start, size):
        for kind in (0, 1):
            for way in (1, -1):
                first[kind, start, 2 * way].wait_recv()
                block = lax.rem(where[kind] - 2 * way + side, side)
                part = refs[kind].at[block, pl.ds(start, size)]
                if (start < half) == (way == 1):
                    second.append(go(part, part, to_ring(kind, 2 * way)))
                second.append(go(part, part, to_ring(kind, way)))

    for offset in far_first(side):
        for kind in (0, 1):
            slot = slot_of(side - offset, side)
            near[kind, slot] = go(
                refs[kind].at[where[kind], 0],
                refs[kind].at[where[kind], slot],
                near_peer[kind](y, z, side, offset),
            )
    own = sgeo_ref.at[rcv]
    across = [go(own, own, peer_r(rcv, n_rcv, o)) for o in range(1, n_rcv)]
    step_one(*pieces[0])
    for index in range(1, len(pieces)):
        step_one(*pieces[index])
        step_two(*pieces[index - 1])
    step_two(*pieces[-1])

    for copy in loads[4:]:
        copy.wait()
    ageo_ref[...] = turned(geometric(as_ref[...], ar_ref[...]))
    send_row = jnp.sum(turned(jnp.exp(ss_ref[0] - sr_ref[0])), axis=0, keepdims=True)
    recv_row = jnp.sum(turned(jnp.exp(rs_ref[0] - rr_ref[0])), axis=0, keepdims=True)
    row_id = lax.broadcasted_iota(jnp.int32, (16, lanes), 0)
    totals = jnp.zeros((16, lanes), f32)
    for index, row in enumerate(split3(send_row) + split3(recv_row)):
        totals = jnp.where(row_id == index, row, totals)
    act_chunk = actions // n_rcv
    for chunk in range(n_rcv):
        act_own[chunk, act_chunk:] = totals
    send_slots[slots] = jnp.zeros(send_slots.shape[1:], f32)
    recv_slots[slots] = jnp.zeros(recv_slots.shape[1:], f32)

    def link(slot, carry):
        b, c = sid[0, 0, slot], rid[0, 0, slot]
        before_b, before_c = jnp.int32(slots), jnp.int32(slots)
        for other in range(slots):
            earlier = other < slot
            before_b = jnp.where((sid[0, 0, other] == b) & earlier, other, before_b)
            before_c = jnp.where((rid[0, 0, other] == c) & earlier, other, before_c)
        prev[0, slot] = before_b
        prev[1, slot] = before_c
        return carry

    def final(ids, table):
        def body(block, carry):
            found = jnp.int32(slots)
            for other in range(slots):
                found = jnp.where(ids[0, 0, other] == block, other, found)
            table[block] = found
            return carry

        return body

    lax.fori_loop(0, slots, link, 0)
    lax.fori_loop(0, blocks, final(rid, last_recv), 0)
    lax.fori_loop(0, send_blocks, final(sid, last_send), 0)

    for (kind, start, distance), copy in first.items():
        if abs(distance) == 1:
            copy.wait_recv()
    for copy in second:
        copy.wait_recv()
    for copy in across:
        copy.wait_recv()
    for copy in count_loads:
        copy.wait()

    live_count = fill[0, 0]

    def one_tile(slot):
        b, c, a = sid[0, 0, slot], rid[0, 0, slot], aid[0, 0, slot]
        live = jnp.where(slot < live_count, 1.0, 0.0).astype(f32)
        begin = c * span
        ty, tz = begin // side, lax.rem(begin, side)
        down = slot_at(ty - y, side)
        recv = jnp.concatenate(
            [
                jnp.concatenate(
                    [top_ref[ty, slot_at(tz + e - z, side)] for e in range(span)], axis=1
                ),
                jnp.concatenate([low_ref[tz + e, down] for e in range(span)], axis=1),
            ],
            axis=0,
        )
        recv_pad = jnp.concatenate([recv, jnp.zeros((lanes - rank, edge), bf16)], axis=0)
        sender = sgeo_ref[pl.ds(b * span, span)].reshape(edge, lanes)
        scaled = (sender.astype(f32) * ageo_ref[pl.ds(a, 1), :]).astype(bf16)
        expected = jnp.dot(scaled, recv_pad, preferred_element_type=f32)
        ratios = (counts[slot].astype(f32) * live / expected).astype(bf16)
        toward_send = lax.dot_general(
            ratios, recv_pad, (((1,), (1,)), ((), ())), preferred_element_type=f32
        )
        toward_recv = lax.dot_general(
            scaled, ratios, (((0,), (0,)), ((), ())), preferred_element_type=f32
        )
        send_term = scaled.astype(f32) * toward_send
        recv_term = recv.astype(f32) * toward_recv[:rank]
        return send_term, recv_term, jnp.sum(send_term, axis=0, keepdims=True)

    def one_group(group, carry):
        done = [one_tile(group * unroll + u) for u in range(unroll)]
        for u, (send_term, recv_term, act_term) in enumerate(done):
            slot = group * unroll + u
            send_slots[slot] = send_term + send_slots[prev[0, slot]]
            recv_slots[slot] = recv_term + recv_slots[prev[1, slot]]
            act_rows[pl.ds(slot, 1), :] = act_term
        return carry

    lax.fori_loop(0, slots // unroll, one_group, 0)

    action_id = lax.broadcasted_iota(jnp.int32, (actions, slots), 0)
    onehot = jnp.where(action_id == aid_row[0], 1.0, 0.0).astype(f32)
    act_sum = jnp.dot(
        onehot, act_rows[...], preferred_element_type=f32, precision=lax.Precision.HIGHEST
    )
    for chunk in range(n_rcv):
        act_own[chunk, :act_chunk] = act_sum[chunk * act_chunk : (chunk + 1) * act_chunk]
    act_copies = []
    for o in range(1, n_rcv):
        other = lax.rem(rcv + o, n_rcv)
        act_copies.append(go(act_own.at[other], act_dst.at[rcv], {"rcv": other}))
    act_dst[rcv] = act_own[rcv]

    def hand_over(block, carry):
        value = recv_slots[last_recv[block]].astype(bf16)
        begin = block * span
        ty, tz = begin // side, lax.rem(begin, side)
        for e in range(span):
            columns = value[:, e * lanes : (e + 1) * lanes]
            parts[0, ty, slot_at(tz + e - z, side)] = columns[:rows]
            parts[1, tz + e, slot_at(ty - y, side)] = columns[rows:]
        return carry

    lax.fori_loop(0, blocks, hand_over, 0)

    came1, came2, came3, came4 = {}, {}, {}, {}

    def block_at(kind, distance):
        return lax.rem(where[kind] + distance + side, side)

    def piece_of(kind, distance, start, size):
        return parts.at[kind, block_at(kind, distance), pl.ds(start, size)]

    backwards = pieces[::-1]
    for start, size in backwards:
        for kind in (0, 1):
            for way in (1, -1):
                at = (kind, (1 - way) // 2, pl.ds(start, size))
                if (start < half) == (way == 1):
                    came4[kind, start, way] = go(
                        piece_of(kind, 4 * way, start, size), from4.at[at], to_ring(kind, 2 * way)
                    )
                came3[kind, start, way] = go(
                    piece_of(kind, 3 * way, start, size), from3.at[at], to_ring(kind, way)
                )
    for start, size in backwards:
        for kind in (0, 1):
            for way in (1, -1):
                at = (kind, (1 - way) // 2, pl.ds(start, size))
                came1[kind, start, way] = go(
                    piece_of(kind, way, start, size), from1.at[at], to_ring(kind, way)
                )

    def give(block, carry):
        value = send_slots[last_send[block]].astype(bf16)
        for e in range(span):
            send_part[block * span + e] = value[e * lanes : (e + 1) * lanes]
        return carry

    lax.fori_loop(0, send_blocks, give, 0)
    send_copies = []
    for o in range(1, n_rcv):
        other = lax.rem(rcv + o, n_rcv)
        send_copies.append(go(send_part.at[other], send_dst.at[rcv], {"rcv": other}))
    send_dst[rcv] = send_part[rcv]

    def join(start, size):
        for kind in (0, 1):
            for way in (1, -1):
                at = (kind, (1 - way) // 2, pl.ds(start, size))
                total = parts[kind, block_at(kind, 2 * way), pl.ds(start, size)].astype(f32)
                came3[kind, start, way].wait_recv()
                total = total + from3[at].astype(f32)
                if (start < half) == (way == 1):
                    came4[kind, start, way].wait_recv()
                    total = total + from4[at].astype(f32)
                joined[at] = total.astype(bf16)
                came2[kind, start, way] = go(joined.at[at], from2.at[at], to_ring(kind, 2 * way))

    def total_of(ref, count):
        value = ref[0].astype(f32)
        for index in range(1, count):
            value = value + ref[index].astype(f32)
        return value

    def spread(level, value):
        me = where[level]
        sum_src[level] = value.astype(bf16)
        sum_dst[level, me] = value.astype(bf16)
        return [
            go(sum_src.at[level], sum_dst.at[level, me], to_ring(level, o))
            for o in far_first(side)
        ]

    def split_totals(value):
        tail = value[act_chunk:]
        result = jnp.zeros_like(tail)
        for base in (0, 3):
            row = tail[base : base + 1] + (tail[base + 1 : base + 2] + tail[base + 2 : base + 3])
            for index, part in enumerate(split3(row)):
                result = jnp.where(row_id == base + index, part, result)
        return jnp.concatenate([value[:act_chunk], result], axis=0)

    near_copies = []

    def finish(start, size):
        for kind in (0, 1):
            total = parts[kind, where[kind], pl.ds(start, size)].astype(f32)
            for way in (1, -1):
                at = (kind, (1 - way) // 2, pl.ds(start, size))
                came1[kind, start, way].wait_recv()
                total = total + from1[at].astype(f32)
                came2[kind, start, way].wait_recv()
                total = total + from2[at].astype(f32)
            near_src[kind, pl.ds(start, size)] = total.astype(bf16)
            for offset in far_first(side):
                slot = slot_of(offset, side)
                if start <= slot < start + size:
                    near_copies.append(
                        go(
                            near_src.at[kind, slot],
                            near_dst.at[kind, slot_of(side - offset, side)],
                            near_peer[kind](y, z, side, offset),
                        )
                    )

    join(*backwards[0])
    join(*backwards[1])
    for copy in act_copies:
        copy.wait_recv()
    sums = spread(0, split_totals(total_of(act_dst, n_rcv)))
    join(*backwards[2])
    join(*backwards[3])
    finish(*backwards[0])
    finish(*backwards[1])
    for copy in sums:
        copy.wait_recv()
    sums = spread(1, split_totals(total_of(sum_dst.at[0], side)))
    finish(*backwards[2])
    finish(*backwards[3])
    for kind in (0, 1):
        near_dst[kind, 0] = near_src[kind, 0]
    for copy in send_copies:
        copy.wait_recv()
    send_out[...] = total_of(send_dst, n_rcv)
    for copy in sums:
        copy.wait_recv()
    full = total_of(sum_dst.at[1], side)
    act_out[pl.ds(rcv * act_chunk, act_chunk), :] = full[:act_chunk]
    own = act_out.at[pl.ds(rcv * act_chunk, act_chunk), :]
    back = [go(own, own, peer_r(rcv, n_rcv, o)) for o in range(1, n_rcv)]
    tot_out[...] = full[act_chunk:]
    for copy in near_copies:
        copy.wait_recv()
    for kind in (0, 1):
        recv_out[kind * rows : (kind + 1) * rows] = total_of(near_dst.at[kind], side)
    for copy in back:
        copy.wait_recv()
    for copy in go.sent:
        copy.wait_send()


def refresh_kernel(*refs):
    sources, outs, refs = refs[:10], refs[10:16], refs[16:]
    held, load_sem = refs[:10], refs[10]
    for index in range(10):
        pltpu.make_async_copy(sources[index], held[index], load_sem.at[index]).start()
    for index in range(10):
        pltpu.make_async_copy(sources[index], held[index], load_sem.at[index]).wait()
    ss_ref, sr_ref, rs_ref, rr_ref, as_ref, ar_ref, send_ref, recv_ref, act_ref, tot_ref = held
    ss_out, sr_out, rs_out, rr_out, as_out, ar_out = outs
    rank = as_ref.shape[0]
    row = lax.broadcasted_iota(jnp.int32, (rank, lanes), 0)
    col = lax.broadcasted_iota(jnp.int32, (rank, lanes), 1)

    def column(index):
        parts = [tot_ref[pl.ds(index + part, 1), :] for part in range(3)]
        wide = jnp.broadcast_to(parts[0] + (parts[1] + parts[2]), (rank, lanes))
        return jnp.sum(jnp.where(row == col, wide, 0.0), axis=1, keepdims=True)

    send_total, recv_total = column(0), column(3)
    act_total = jnp.sum(jnp.exp(as_ref[...] - ar_ref[...]), axis=1, keepdims=True)
    ss_out[0] = refresh(ss_ref[0], prior_shape + send_ref[...].T[:rank])
    sr_out[0] = refresh(sr_ref[0], prior_rate + recv_total * act_total)
    rs_out[0] = refresh(rs_ref[0], prior_shape + recv_ref[...])
    rr_out[0] = refresh(rr_ref[0], prior_rate + send_total * act_total)
    as_out[...] = refresh(as_ref[...], prior_shape + act_ref[...].T[:rank])
    ar_out[...] = refresh(ar_ref[...], prior_rate + send_total * recv_total)


def per_device(
    side,
    n_rcv,
    tile_counts,
    tile_sender,
    tile_receiver,
    tile_action,
    tile_fill,
    ss,
    sr,
    rs,
    rr,
    ash,
    art,
):
    rank, actions = ash.shape
    slots, edge = tile_counts.shape[2], tile_counts.shape[3]
    rows, span = rank // 2, edge // lanes
    blocks, send_blocks = side * side // span, n_rcv // span
    vmem = pl.BlockSpec(memory_space=pltpu.VMEM)
    hbm = pl.BlockSpec(memory_space=pltpu.HBM)
    shape = jax.ShapeDtypeStruct
    dma = pltpu.SemaphoreType.DMA
    own, act = pltpu.VMEM(ss.shape, f32), pltpu.VMEM(ash.shape, f32)
    ids = pltpu.SMEM(tile_sender.shape, jnp.int32)
    geo = pltpu.VMEM((side, side, rows, lanes), bf16)
    landing = pltpu.VMEM((2, 2, side, rows, lanes), bf16)
    near = pltpu.VMEM((2, side, rows, lanes), bf16)
    sender = pltpu.VMEM((n_rcv, lanes, lanes), bf16)
    chunk = actions // n_rcv + 16

    recv_stat, send_stat, act_stat, totals = pl.pallas_call(
        functools.partial(fused_kernel, side, n_rcv),
        out_shape=(
            shape((rank, lanes), f32),
            shape((lanes, lanes), f32),
            shape((actions, lanes), f32),
            shape((16, lanes), f32),
        ),
        in_specs=[hbm] * 11,
        out_specs=(vmem,) * 4,
        scratch_shapes=[
            own,
            own,
            own,
            own,
            act,
            act,
            ids,
            ids,
            ids,
            pltpu.SMEM(tile_fill.shape, jnp.int32),
            pltpu.VMEM(tile_action.shape, jnp.int32),
            pltpu.SMEM((2, slots), jnp.int32),
            pltpu.SMEM((blocks,), jnp.int32),
            pltpu.SMEM((send_blocks,), jnp.int32),
            pltpu.VMEM((slots, edge, edge), bf16),
            geo,
            geo,
            sender,
            pltpu.VMEM((actions, lanes), f32),
            pltpu.VMEM((slots + 1, edge, lanes), f32),
            pltpu.VMEM((slots + 1, rank, edge), f32),
            pltpu.VMEM((slots, lanes), f32),
            pltpu.VMEM((2, side, side, rows, lanes), bf16),
            landing,
            landing,
            landing,
            landing,
            landing,
            near,
            near,
            sender,
            sender,
            pltpu.VMEM((n_rcv, chunk, lanes), f32),
            pltpu.VMEM((n_rcv, chunk, lanes), f32),
            pltpu.VMEM((2, chunk, lanes), bf16),
            pltpu.VMEM((2, side, chunk, lanes), bf16),
            dma((11,)),
            dma((slots // unroll,)),
            dma((16, 16)),
            dma((16, 16)),
        ],
        compiler_params=pltpu.CompilerParams(
            collective_id=0, has_side_effects=True, vmem_limit_bytes=whole_vmem
        ),
    )(
        tile_counts,
        tile_sender,
        tile_receiver,
        tile_action,
        tile_fill,
        ss,
        sr,
        rs,
        rr,
        ash,
        art,
    )

    sources = (ss, sr, rs, rr, ash, art, send_stat, recv_stat, act_stat, totals)
    return pl.pallas_call(
        refresh_kernel,
        out_shape=tuple(shape(x.shape, f32) for x in (ss, sr, rs, rr, ash, art)),
        in_specs=[hbm] * len(sources),
        out_specs=(vmem,) * 6,
        scratch_shapes=[pltpu.VMEM(x.shape, f32) for x in sources] + [dma((len(sources),))],
        compiler_params=pltpu.CompilerParams(vmem_limit_bytes=whole_vmem),
    )(*sources)


def solution(mesh):
    n_snd, n_rcv = mesh.shape["snd"], mesh.shape["rcv"]
    side = round(n_snd**0.5)
    return jax.shard_map(
        functools.partial(per_device, side, n_rcv),
        mesh=mesh,
        in_specs=(
            P("snd", "rcv", None, None, None),
            P("snd", "rcv", None),
            P("snd", "rcv", None),
            P("snd", "rcv", None),
            P("snd", "rcv"),
            P("snd", None, "rcv"),
            P("snd", None, "rcv"),
            P("rcv", None, "snd"),
            P("rcv", None, "snd"),
            P(),
            P(),
        ),
        out_specs=(
            P("snd", None, "rcv"),
            P("snd", None, "rcv"),
            P("rcv", None, "snd"),
            P("rcv", None, "snd"),
            P(),
            P(),
        ),
        check_vma=False,
    )
```

time: 1050 us -> 75.8 us (0.07)
  waiting for transfers between devices: 567 us -> 0 us
  blocking collectives: 134 us -> 0 us
  other arithmetic: 114 us -> 0 us
  loops' own time: 98.8 us -> 0 us
  local copies, waits for them, and re-layouts: 83.5 us -> 0 us
  Pallas kernels: 0 us -> 74.4 us
  matrix products: 28.9 us -> 0 us
  between operations: 14.6 us -> 1.29 us
    psum x1 -> x0, waiting for transfers between devices: 256 us -> none  [per_device(): action_stat = lax.psum(act_term, ('snd', 'rcv'))]
    reduce_scatter x1 -> x0, waiting for transfers between devices: 244 us -> none  [per_device(): lax.psum_scatter(recv_term, 'snd', scatter_dimension=1, tiled=True)]
    psum x1 -> x0, blocking collectives: 107 us -> none  [per_device(): lax.psum((sender_part, receiver_part), ('snd', 'rcv'))]
    another operation x1 -> x0, loops' own time: 98.8 us -> none  [per_device(): lax.fori_loop(0, turns_needed, one_turn, initial)]
    pallas_call x0 -> x2, Pallas kernels: none -> 74.4 us  [the longest x1 72.2 us: per_device(): pl.pallas_call(functools.partial(fused_kernel, side, n_rcv), out_shape=(s...]
    dynamic_update_slice x56 -> x0, other arithmetic: 51.9 us -> none  [add_columns(): lax.dynamic_update_slice_in_dim(running, current + addend, start_col, 1)]
    dynamic_update_slice x32 -> x0, local copies, waits for them, and re-layouts: 40.9 us -> none  [add_columns(): lax.dynamic_update_slice_in_dim(running, current + addend, start_col, 1)]
    add x32 -> x0, other arithmetic: 38.1 us -> none  [add_columns(): current + addend]
  transfers between devices with their start and end apart: 5 -> 0, of which waited for: 4 -> 0; matrix products, arithmetic and copies ran while one was open for 1% -> 0% of each run, Pallas kernels for 0% -> 0%
where the time goes in v2:
time: 75.8 us; the launch traced here: 75.6 us
  Pallas kernels  74.4 us (98%)
  between operations  1.29 us (2%)
    pallas_call x1, Pallas kernels, per_device(): pl.pallas_call(functools.partial(fused_kernel, side, n_rcv), out_shape=(s...  72.2 us
    pallas_call x1, Pallas kernels, per_device(): pl.pallas_call(refresh_kernel, out_shape=tuple((shape(x.shape, f32) for x...  2.14 us

profile of v2, /device:TPU:1, one launch (start us, length us, event | category | flops | bytes accessed | tf_op | source)
XLA Modules:
  0.0 75.6 jit_solution(3716617471581216638)
XLA Ops:
  1.3 72.2 %shard_map.154 = (f32[96,128]{1,0:T(8,128)}, f32[128,128]{1,0:T(8,128)}, f32[256,128]{1,0:T(8,128)}, f32[16,128]{1,0:T(8,128)}) custom-call(bf16[1,1,32,256,256]{4,3,2,1,0:T(8,128)(2,1)} %counts_hbm.1, s32[1,1,32]{2,1,0:T(1,128)} %sid_hbm.1, s32[1,1,32]{2,1,0:T(1,128)} %rid_hbm.1, s32[1,1,32]{2,1,0:T(1,128)} %aid_hbm.1, s32[1,1]{1,0:T(1,128)S(6)} %copy.17.fill_hbm, ...), custom_call_target="tpu_custom_call" | custom-call | tf_op jit(solution)/shard_map/pallas_call | solution.py:586
  73.5 2.1 %shard_map.155 = (f32[1,96,128]{2,1,0:T(8,128)}, f32[1,96,128]{2,1,0:T(8,128)}, f32[1,96,128]{2,1,0:T(8,128)}, f32[1,96,128]{2,1,0:T(8,128)}, f32[96,256]{1,0:T(8,128)}, /*index=5*/f32[96,256]{1,0:T(8,128)}) custom-call(f32[1,96,128]{2,1,0:T(8,128)} %refs_0_.1, f32[1,96,128]{2,1,0:T(8,128)} %refs_1_.1, f32[1,96,128]{2,1,0:T(8,128)} %refs_2_.1, ...), custom_call_target="tpu_custom_call" | custom-call | tf_op jit(solution)/shard_map/pallas_call | solution.py:656

commit v3 on v2

v3 whole, which is shorter than its diff:
```python
import functools

import jax
import jax.numpy as jnp
from jax import lax
from jax.experimental import pallas as pl
from jax.experimental.pallas import tpu as pltpu
from jax.sharding import PartitionSpec as P

prior_shape = 0.3
prior_rate = 0.3
step_size = 0.5
lanes = 128
unroll = 8
whole_vmem = 60 << 20

MESH = pl.DeviceIdType.MESH
bf16 = jnp.bfloat16
f32 = jnp.float32


def digamma_series(value):
    shift_sum = jnp.zeros_like(value)
    for offset in range(6):
        shift_sum = shift_sum + 1.0 / (value + float(offset))
    moved = value + 6.0
    inverse = 1.0 / moved
    inv_square = inverse * inverse
    series = (
        jnp.log(moved)
        - 0.5 * inverse
        - inv_square * (1.0 / 12.0 - inv_square * (1.0 / 120.0 - inv_square / 252.0))
    )
    return series - shift_sum


def geometric(log_shape, log_rate):
    return jnp.exp(digamma_series(jnp.exp(log_shape)) - log_rate)


def refresh(log_value, target):
    return jnp.log((1.0 - step_size) * jnp.exp(log_value) + step_size * target)


def turned(value):
    rank, cols = value.shape
    padded = jnp.concatenate([value, jnp.zeros((lanes - rank, cols), value.dtype)], axis=0)
    return padded.T


def place(side):
    snd = lax.axis_index("snd")
    return snd // side, lax.rem(snd, side), lax.axis_index("rcv")


def peer_y(y, z, side, offset):
    return {"snd": lax.rem(y + offset + side, side) * side + z}


def peer_z(y, z, side, offset):
    return {"snd": y * side + lax.rem(z + offset + side, side)}


def peer_r(rcv, n_rcv, offset):
    return {"rcv": lax.rem(rcv + offset, n_rcv)}


def greet(side, n_rcv):
    y, z, rcv = place(side)
    barrier = pltpu.get_barrier_semaphore()
    for offset in far_first(side):
        for peer in (peer_y, peer_z):
            pl.semaphore_signal(
                barrier, inc=1, device_id=peer(y, z, side, offset), device_id_type=MESH
            )
    for offset in range(1, n_rcv):
        pl.semaphore_signal(
            barrier, inc=1, device_id=peer_r(rcv, n_rcv, offset), device_id_type=MESH
        )
    return barrier, 2 * (side - 1) + n_rcv - 1


def far_first(side):
    return sorted(range(1, side), key=lambda o: -min(o, side - o))


def slot_of(offset, side):
    return 0 if offset == 0 else (2 * offset - 1 if offset <= side // 2 else 2 * (side - offset))


def slot_at(offset, side):
    offset = lax.rem(offset + side, side)
    near = jnp.maximum(2 * offset - 1, 0)
    return jnp.where(offset <= side // 2, near, 2 * (side - offset))


class Group:
    def __init__(self, sems):
        self.sems = sems

    def start(self, src, dst, device, arrive=None):
        pltpu.make_async_remote_copy(
            src_ref=src,
            dst_ref=dst,
            send_sem=self.sems[0],
            recv_sem=arrive if arrive is not None else self.sems[1],
            device_id=device,
            device_id_type=MESH,
        ).start()


def settle(sem, like):
    pltpu.make_async_copy(like, like, sem).wait()


def split3(value):
    high = value.astype(bf16).astype(f32)
    middle = (value - high).astype(bf16).astype(f32)
    return high, middle, value - high - middle


def fused_kernel(
    side,
    n_rcv,
    counts_hbm,
    sid_hbm,
    rid_hbm,
    aid_hbm,
    fill_hbm,
    ss_hbm,
    sr_hbm,
    rs_hbm,
    rr_hbm,
    as_hbm,
    ar_hbm,
    recv_out,
    send_out,
    act_out,
    tot_out,
    own_ref,
    act_ref,
    ids,
    fill,
    aid_row,
    prev,
    last_recv,
    last_send,
    counts,
    top_ref,
    low_ref,
    sgeo_ref,
    ageo_ref,
    scaled_ref,
    turned_ref,
    send_slots,
    recv_slots,
    act_rows,
    parts,
    from1,
    from2,
    from3,
    from4,
    joined,
    near_src,
    near_dst,
    send_part,
    send_dst,
    act_own,
    act_dst,
    sum_src,
    sum_dst,
    load_sem,
    near_sems,
    ring_send,
    ring_recv,
    rest_recv,
    done_recv,
    last_sems,
    pair_sems,
):
    y, z, rcv = place(side)
    half = side // 2
    slots, edge = counts.shape[0], counts.shape[1]
    span = edge // lanes
    rank, rows = own_ref.shape[1], top_ref.shape[2]
    actions = ageo_ref.shape[0]
    blocks, send_blocks = side * side // span, n_rcv // span

    loads = [
        pltpu.make_async_copy(src, dst, load_sem.at[index])
        for index, src, dst in (
            (0, rs_hbm.at[0], own_ref.at[0]),
            (0, rr_hbm.at[0], own_ref.at[1]),
            (0, ss_hbm.at[0], own_ref.at[2]),
            (0, sr_hbm.at[0], own_ref.at[3]),
            (1, as_hbm, act_ref.at[0]),
            (1, ar_hbm, act_ref.at[1]),
            (2, sid_hbm.at[0], ids.at[0]),
            (2, rid_hbm.at[0], ids.at[1]),
            (2, aid_hbm.at[0], ids.at[2]),
            (3, fill_hbm, fill),
            (4, aid_hbm.at[0], aid_row),
            (5, counts_hbm.at[0, 0], counts),
        )
    ]
    for copy in loads:
        copy.start()
    barrier, greeted = greet(side, n_rcv)
    settle(load_sem.at[0], own_ref)
    geo = geometric(own_ref[0], own_ref[1]).astype(bf16)
    top_ref[y, 0] = geo[:rows]
    low_ref[z, 0] = geo[rows:]
    sgeo_ref[rcv] = turned(geometric(own_ref[2], own_ref[3])).astype(bf16)
    pl.semaphore_wait(barrier, greeted)

    refs, where = (top_ref, low_ref), (y, z)
    ring_peer, near_peer = (peer_y, peer_z), (peer_z, peer_y)
    pieces = ((0, 1), (1, half - 1), (half, side - half))

    def to_ring(kind, distance):
        return ring_peer[kind](y, z, side, distance)

    def block_at(kind, distance):
        return lax.rem(where[kind] + distance + side, side)

    near = [Group((near_sems.at[kind, 0], None)) for kind in (0, 1)]
    ring = [Group((ring_send.at[0, kind], rest_recv.at[kind])) for kind in (0, 1)]

    def forward(index):
        start, size = pieces[index]
        for kind in (0, 1):
            part = refs[kind].at[where[kind], pl.ds(start, size)]
            if start:
                settle(near_sems.at[kind, index], part)
            for way in (0, 1):
                ring[kind].start(
                    part, part, to_ring(kind, 2 - 4 * way), ring_recv.at[0, kind, way, index]
                )

    def onward(index):
        start, size = pieces[index]
        for kind in (0, 1):
            for way in (0, 1):
                sign = 1 - 2 * way
                part = refs[kind].at[block_at(kind, -2 * sign), pl.ds(start, size)]
                settle(ring_recv.at[0, kind, way, index], part)
                if (start < half) == (way == 0):
                    ring[kind].start(part, part, to_ring(kind, 2 * sign))
                ring[kind].start(part, part, to_ring(kind, sign))

    for offset in far_first(side):
        for kind in (0, 1):
            slot = slot_of(side - offset, side)
            near[kind].start(
                refs[kind].at[where[kind], 0],
                refs[kind].at[where[kind], slot],
                near_peer[kind](y, z, side, offset),
                near_sems.at[kind, 1 if slot < half else 2],
            )
    forward(0)
    across = Group((pair_sems.at[0, 0], pair_sems.at[0, 1]))
    for o in range(1, n_rcv):
        across.start(sgeo_ref.at[rcv], sgeo_ref.at[rcv], peer_r(rcv, n_rcv, o))

    settle(load_sem.at[1], act_ref)
    settle(load_sem.at[2], ids)
    ageo_ref[...] = turned(geometric(act_ref[0], act_ref[1]))

    def link(slot, carry):
        b, c = ids[0, 0, slot], ids[1, 0, slot]
        before_b, before_c = jnp.int32(slots), jnp.int32(slots)
        for other in range(slots):
            earlier = other < slot
            before_b = jnp.where((ids[0, 0, other] == b) & earlier, other, before_b)
            before_c = jnp.where((ids[1, 0, other] == c) & earlier, other, before_c)
        prev[0, slot] = before_b
        prev[1, slot] = before_c
        return carry

    def final(row, table):
        def body(block, carry):
            found = jnp.int32(slots)
            for other in range(slots):
                found = jnp.where(ids[row, 0, other] == block, other, found)
            table[block] = found
            return carry

        return body

    lax.fori_loop(0, slots, link, 0)
    for index in range(1, len(pieces)):
        forward(index)
    for index in range(len(pieces)):
        onward(index)
    for kind in (0, 1):
        part = refs[kind].at[where[kind]]
        for sign in (1, -1):
            ring[kind].start(part, part, to_ring(kind, sign))

    settle(pair_sems.at[0, 1], sgeo_ref.at[pl.ds(0, n_rcv - 1)])

    def scale(slot, carry):
        b, a = ids[0, 0, slot], ids[2, 0, slot]
        sender = sgeo_ref[pl.ds(b * span, span)].reshape(edge, lanes)
        scaled = (sender.astype(f32) * ageo_ref[pl.ds(a, 1), :]).astype(bf16)
        scaled_ref[slot] = scaled
        turned_ref[slot] = scaled.T[:rank]
        return carry

    lax.fori_loop(0, slots, scale, 0, unroll=4)
    lax.fori_loop(0, blocks, final(1, last_recv), 0)
    lax.fori_loop(0, send_blocks, final(0, last_send), 0)
    send_row = jnp.sum(turned(jnp.exp(own_ref[2] - own_ref[3])), axis=0, keepdims=True)
    recv_row = jnp.sum(turned(jnp.exp(own_ref[0] - own_ref[1])), axis=0, keepdims=True)
    row_id = lax.broadcasted_iota(jnp.int32, (16, lanes), 0)
    totals = jnp.zeros((16, lanes), f32)
    for index, row in enumerate(split3(send_row) + split3(recv_row)):
        totals = jnp.where(row_id == index, row, totals)
    act_chunk = actions // n_rcv
    for chunk in range(n_rcv):
        act_own[chunk, act_chunk:] = totals.astype(bf16)
    send_slots[slots] = jnp.zeros(send_slots.shape[1:], f32)
    recv_slots[slots] = jnp.zeros(recv_slots.shape[1:], f32)
    settle(load_sem.at[3], fill)
    settle(load_sem.at[4], aid_row)
    settle(load_sem.at[5], counts)
    for kind in (0, 1):
        settle(rest_recv.at[kind], refs[kind].at[pl.ds(0, 5)])

    live_count = fill[0, 0]

    def one_tile(slot):
        c = ids[1, 0, slot]
        live = jnp.where(slot < live_count, 1.0, 0.0).astype(f32)
        begin = c * span
        ty, tz = begin // side, lax.rem(begin, side)
        down = slot_at(ty - y, side)
        recv = jnp.concatenate(
            [
                jnp.concatenate(
                    [top_ref[ty, slot_at(tz + e - z, side)] for e in range(span)], axis=1
                ),
                jnp.concatenate([low_ref[tz + e, down] for e in range(span)], axis=1),
            ],
            axis=0,
        )
        recv_pad = jnp.concatenate([recv, jnp.zeros((lanes - rank, edge), bf16)], axis=0)
        scaled = scaled_ref[slot]
        expected = jnp.dot(scaled, recv_pad, preferred_element_type=f32)
        ratios = (counts[slot].astype(f32) * live / expected).astype(bf16)
        toward_send = lax.dot_general(
            ratios, recv_pad, (((1,), (1,)), ((), ())), preferred_element_type=f32
        )
        toward_recv = jnp.dot(turned_ref[slot], ratios, preferred_element_type=f32)
        send_term = scaled.astype(f32) * toward_send
        recv_term = recv.astype(f32) * toward_recv
        return send_term, recv_term, jnp.sum(send_term, axis=0, keepdims=True)

    def one_group(group, carry):
        done = [one_tile(group * unroll + u) for u in range(unroll)]
        for u, (send_term, recv_term, act_term) in enumerate(done):
            slot = group * unroll + u
            send_slots[slot] = send_term + send_slots[prev[0, slot]]
            recv_slots[slot] = recv_term + recv_slots[prev[1, slot]]
            act_rows[pl.ds(slot, 1), :] = act_term
        return carry

    lax.fori_loop(0, slots // unroll, one_group, 0)

    action_id = lax.broadcasted_iota(jnp.int32, (actions, slots), 0)
    onehot = jnp.where(action_id == aid_row[...], 1.0, 0.0).astype(f32)
    act_sum = jnp.dot(
        onehot, act_rows[...], preferred_element_type=f32, precision=lax.Precision.HIGHEST
    )
    for chunk in range(n_rcv):
        act_own[chunk, :act_chunk] = act_sum[chunk * act_chunk : (chunk + 1) * act_chunk].astype(
            bf16
        )
    acts = Group((pair_sems.at[1, 0], pair_sems.at[1, 1]))
    for o in range(1, n_rcv):
        other = lax.rem(rcv + o, n_rcv)
        acts.start(act_own.at[other], act_dst.at[rcv], {"rcv": other})
    act_dst[rcv] = act_own[rcv]

    def hand_over(block, carry):
        value = recv_slots[last_recv[block]].astype(bf16)
        begin = block * span
        ty, tz = begin // side, lax.rem(begin, side)
        for e in range(span):
            columns = value[:, e * lanes : (e + 1) * lanes]
            parts[0, ty, slot_at(tz + e - z, side)] = columns[:rows]
            parts[1, tz + e, slot_at(ty - y, side)] = columns[rows:]
        return carry

    lax.fori_loop(0, blocks, hand_over, 0, unroll=2)

    def piece_of(kind, distance, start, size):
        return parts.at[kind, block_at(kind, distance), pl.ds(start, size)]

    out_ring = [Group((ring_send.at[1, kind], None)) for kind in (0, 1)]
    backwards = tuple(reversed(range(len(pieces))))

    def far_parts(index):
        start, size = pieces[index]
        for kind in (0, 1):
            for way in (0, 1):
                sign = 1 - 2 * way
                at = (kind, way, pl.ds(start, size))
                arrive = ring_recv.at[1, kind, way, index]
                if (start < half) == (way == 0):
                    out_ring[kind].start(
                        piece_of(kind, 4 * sign, start, size),
                        from4.at[at],
                        to_ring(kind, 2 * sign),
                        arrive,
                    )
                out_ring[kind].start(
                    piece_of(kind, 3 * sign, start, size), from3.at[at], to_ring(kind, sign), arrive
                )

    def join(index):
        start, size = pieces[index]
        for kind in (0, 1):
            for way in (0, 1):
                sign = 1 - 2 * way
                at = (kind, way, pl.ds(start, size))
                both = (start < half) == (way == 0)
                settle(
                    ring_recv.at[1, kind, way, index],
                    parts.at[0, 0, pl.ds(0, size * (2 if both else 1))],
                )
                total = parts[kind, block_at(kind, 2 * sign), pl.ds(start, size)].astype(f32)
                total = total + from3[at].astype(f32)
                if both:
                    total = total + from4[at].astype(f32)
                joined[at] = total.astype(bf16)
                out_ring[kind].start(
                    joined.at[at], from2.at[at], to_ring(kind, 2 * sign), done_recv.at[kind, index]
                )
        for kind in (0, 1):
            for way in (0, 1):
                sign = 1 - 2 * way
                out_ring[kind].start(
                    piece_of(kind, sign, start, size),
                    from1.at[kind, way, pl.ds(start, size)],
                    to_ring(kind, sign),
                    done_recv.at[kind, index],
                )

    def total_of(ref, count):
        value = ref[0].astype(f32)
        for index in range(1, count):
            value = value + ref[index].astype(f32)
        return value

    def spread(level, value):
        me = where[level]
        sum_src[level] = value.astype(bf16)
        sum_dst[level, me] = value.astype(bf16)
        group = Group((pair_sems.at[2 + level, 0], pair_sems.at[2 + level, 1]))
        for o in far_first(side):
            group.start(sum_src.at[level], sum_dst.at[level, me], to_ring(level, o))

    def split_totals(value):
        tail = value[act_chunk:]
        result = jnp.zeros_like(tail)
        for base in (0, 3):
            row = tail[base : base + 1] + (tail[base + 1 : base + 2] + tail[base + 2 : base + 3])
            for index, part in enumerate(split3(row)):
                result = jnp.where(row_id == base + index, part, result)
        return jnp.concatenate([value[:act_chunk], result], axis=0)

    last = [Group((last_sems.at[kind, 0], last_sems.at[kind, 1])) for kind in (0, 1)]

    def finish(index):
        start, size = pieces[index]
        for kind in (0, 1):
            settle(done_recv.at[kind, index], parts.at[0, pl.ds(0, size), pl.ds(0, 4)])
            total = parts[kind, where[kind], pl.ds(start, size)].astype(f32)
            for way in (0, 1):
                at = (kind, way, pl.ds(start, size))
                total = total + from1[at].astype(f32) + from2[at].astype(f32)
            near_src[kind, pl.ds(start, size)] = total.astype(bf16)
            for offset in far_first(side):
                slot = slot_of(offset, side)
                if start <= slot < start + size:
                    last[kind].start(
                        near_src.at[kind, slot],
                        near_dst.at[kind, slot_of(side - offset, side)],
                        near_peer[kind](y, z, side, offset),
                    )

    for index in backwards:
        far_parts(index)

    def give(block, carry):
        value = send_slots[last_send[block]].astype(bf16)
        for e in range(span):
            send_part[block * span + e] = value[e * lanes : (e + 1) * lanes]
        return carry

    lax.fori_loop(0, send_blocks, give, 0)
    sends = Group((pair_sems.at[4, 0], pair_sems.at[4, 1]))
    for o in range(1, n_rcv):
        other = lax.rem(rcv + o, n_rcv)
        sends.start(send_part.at[other], send_dst.at[rcv], {"rcv": other})
    send_dst[rcv] = send_part[rcv]

    settle(pair_sems.at[1, 1], act_dst.at[pl.ds(0, n_rcv - 1)])
    spread(0, split_totals(total_of(act_dst, n_rcv)))
    for index in backwards:
        join(index)
    settle(pair_sems.at[2, 1], sum_dst.at[0, pl.ds(0, side - 1)])
    spread(1, split_totals(total_of(sum_dst.at[0], side)))
    for index in backwards:
        finish(index)
    for kind in (0, 1):
        near_dst[kind, 0] = near_src[kind, 0]
    settle(pair_sems.at[3, 1], sum_dst.at[1, pl.ds(0, side - 1)])
    full = total_of(sum_dst.at[1], side)
    act_out[pl.ds(rcv * act_chunk, act_chunk), :] = full[:act_chunk]
    own = act_out.at[pl.ds(rcv * act_chunk, act_chunk), :]
    back = Group((pair_sems.at[5, 0], pair_sems.at[5, 1]))
    for o in range(1, n_rcv):
        back.start(own, own, peer_r(rcv, n_rcv, o))
    tot_out[...] = full[act_chunk:]
    settle(pair_sems.at[4, 1], send_dst.at[pl.ds(0, n_rcv - 1)])
    send_out[...] = total_of(send_dst, n_rcv)

    for kind in (0, 1):
        settle(near_sems.at[kind, 0], refs[kind].at[0, pl.ds(0, side - 1)])
        settle(ring_send.at[0, kind], refs[kind].at[pl.ds(0, side - 1)])
        settle(ring_send.at[1, kind], refs[kind].at[pl.ds(0, side - 1)])
    settle(pair_sems.at[0, 0], sgeo_ref.at[pl.ds(0, n_rcv - 1)])
    settle(pair_sems.at[1, 0], act_dst.at[pl.ds(0, n_rcv - 1)])
    settle(pair_sems.at[2, 0], sum_dst.at[0, pl.ds(0, side - 1)])
    settle(pair_sems.at[3, 0], sum_dst.at[1, pl.ds(0, side - 1)])
    settle(pair_sems.at[4, 0], send_dst.at[pl.ds(0, n_rcv - 1)])
    for kind in (0, 1):
        settle(last_sems.at[kind, 1], near_dst.at[kind, pl.ds(0, side - 1)])
        recv_out[kind * rows : (kind + 1) * rows] = total_of(near_dst.at[kind], side)
    for kind in (0, 1):
        settle(last_sems.at[kind, 0], near_dst.at[kind, pl.ds(0, side - 1)])
    for end in (1, 0):
        settle(pair_sems.at[5, end], act_out.at[pl.ds(0, (n_rcv - 1) * act_chunk), :])


def refresh_kernel(*refs):
    sources, outs, refs = refs[:10], refs[10:16], refs[16:]
    held, load_sem = refs[:10], refs[10]
    for index in range(10):
        pltpu.make_async_copy(sources[index], held[index], load_sem.at[index]).start()
    for index in range(10):
        pltpu.make_async_copy(sources[index], held[index], load_sem.at[index]).wait()
    ss_ref, sr_ref, rs_ref, rr_ref, as_ref, ar_ref, send_ref, recv_ref, act_ref, tot_ref = held
    ss_out, sr_out, rs_out, rr_out, as_out, ar_out = outs
    rank = as_ref.shape[0]
    row = lax.broadcasted_iota(jnp.int32, (rank, lanes), 0)
    col = lax.broadcasted_iota(jnp.int32, (rank, lanes), 1)

    def column(index):
        parts = [tot_ref[pl.ds(index + part, 1), :] for part in range(3)]
        wide = jnp.broadcast_to(parts[0] + (parts[1] + parts[2]), (rank, lanes))
        return jnp.sum(jnp.where(row == col, wide, 0.0), axis=1, keepdims=True)

    send_total, recv_total = column(0), column(3)
    act_total = jnp.sum(jnp.exp(as_ref[...] - ar_ref[...]), axis=1, keepdims=True)
    ss_out[0] = refresh(ss_ref[0], prior_shape + send_ref[...].T[:rank])
    sr_out[0] = refresh(sr_ref[0], prior_rate + recv_total * act_total)
    rs_out[0] = refresh(rs_ref[0], prior_shape + recv_ref[...])
    rr_out[0] = refresh(rr_ref[0], prior_rate + send_total * act_total)
    as_out[...] = refresh(as_ref[...], prior_shape + act_ref[...].T[:rank])
    ar_out[...] = refresh(ar_ref[...], prior_rate + send_total * recv_total)


def per_device(
    side,
    n_rcv,
    tile_counts,
    tile_sender,
    tile_receiver,
    tile_action,
    tile_fill,
    ss,
    sr,
    rs,
    rr,
    ash,
    art,
):
    rank, actions = ash.shape
    slots, edge = tile_counts.shape[2], tile_counts.shape[3]
    rows, span = rank // 2, edge // lanes
    blocks, send_blocks = side * side // span, n_rcv // span
    vmem = pl.BlockSpec(memory_space=pltpu.VMEM)
    hbm = pl.BlockSpec(memory_space=pltpu.HBM)
    shape = jax.ShapeDtypeStruct
    dma = pltpu.SemaphoreType.DMA
    geo = pltpu.VMEM((side, side, rows, lanes), bf16)
    landing = pltpu.VMEM((2, 2, side, rows, lanes), bf16)
    near = pltpu.VMEM((2, side, rows, lanes), bf16)
    sender = pltpu.VMEM((n_rcv, lanes, lanes), bf16)
    chunk = actions // n_rcv + 16

    recv_stat, send_stat, act_stat, totals = pl.pallas_call(
        functools.partial(fused_kernel, side, n_rcv),
        out_shape=(
            shape((rank, lanes), f32),
            shape((lanes, lanes), f32),
            shape((actions, lanes), f32),
            shape((16, lanes), f32),
        ),
        in_specs=[hbm] * 11,
        out_specs=(vmem,) * 4,
        scratch_shapes=[
            pltpu.VMEM((4, rank, lanes), f32),
            pltpu.VMEM((2, rank, actions), f32),
            pltpu.SMEM((3, 1, slots), jnp.int32),
            pltpu.SMEM(tile_fill.shape, jnp.int32),
            pltpu.VMEM((1, slots), jnp.int32),
            pltpu.SMEM((2, slots), jnp.int32),
            pltpu.SMEM((blocks,), jnp.int32),
            pltpu.SMEM((send_blocks,), jnp.int32),
            pltpu.VMEM((slots, edge, edge), bf16),
            geo,
            geo,
            sender,
            pltpu.VMEM((actions, lanes), f32),
            pltpu.VMEM((slots, edge, lanes), bf16),
            pltpu.VMEM((slots, rank, edge), bf16),
            pltpu.VMEM((slots + 1, edge, lanes), f32),
            pltpu.VMEM((slots + 1, rank, edge), f32),
            pltpu.VMEM((slots, lanes), f32),
            pltpu.VMEM((2, side, side, rows, lanes), bf16),
            landing,
            landing,
            landing,
            landing,
            landing,
            near,
            near,
            sender,
            sender,
            pltpu.VMEM((n_rcv, chunk, lanes), bf16),
            pltpu.VMEM((n_rcv, chunk, lanes), bf16),
            pltpu.VMEM((2, chunk, lanes), bf16),
            pltpu.VMEM((2, side, chunk, lanes), bf16),
            dma((6,)),
            dma((2, 3)),
            dma((2, 2)),
            dma((2, 2, 2, 3)),
            dma((2,)),
            dma((2, 3)),
            dma((2, 2)),
            dma((6, 2)),
        ],
        compiler_params=pltpu.CompilerParams(
            collective_id=0, has_side_effects=True, vmem_limit_bytes=whole_vmem
        ),
    )(
        tile_counts,
        tile_sender,
        tile_receiver,
        tile_action,
        tile_fill,
        ss,
        sr,
        rs,
        rr,
        ash,
        art,
    )

    sources = (ss, sr, rs, rr, ash, art, send_stat, recv_stat, act_stat, totals)
    return pl.pallas_call(
        refresh_kernel,
        out_shape=tuple(shape(x.shape, f32) for x in (ss, sr, rs, rr, ash, art)),
        in_specs=[hbm] * len(sources),
        out_specs=(vmem,) * 6,
        scratch_shapes=[pltpu.VMEM(x.shape, f32) for x in sources] + [dma((len(sources),))],
        compiler_params=pltpu.CompilerParams(vmem_limit_bytes=whole_vmem),
    )(*sources)


def solution(mesh):
    n_snd, n_rcv = mesh.shape["snd"], mesh.shape["rcv"]
    side = round(n_snd**0.5)
    return jax.shard_map(
        functools.partial(per_device, side, n_rcv),
        mesh=mesh,
        in_specs=(
            P("snd", "rcv", None, None, None),
            P("snd", "rcv", None),
            P("snd", "rcv", None),
            P("snd", "rcv", None),
            P("snd", "rcv"),
            P("snd", None, "rcv"),
            P("snd", None, "rcv"),
            P("rcv", None, "snd"),
            P("rcv", None, "snd"),
            P(),
            P(),
        ),
        out_specs=(
            P("snd", None, "rcv"),
            P("snd", None, "rcv"),
            P("rcv", None, "snd"),
            P("rcv", None, "snd"),
            P(),
            P(),
        ),
        check_vma=False,
    )
```

time: 75.8 us -> 63.9 us (0.84)
  Pallas kernels: 74.4 us -> 62.5 us
    pallas_call x1, Pallas kernels: 72.2 us -> 60.4 us  [per_device(): pl.pallas_call(functools.partial(fused_kernel, side, n_rcv), out_shape=(s...]
where the time goes in v3:
time: 63.9 us; the launch traced here: 63.8 us
  Pallas kernels  62.5 us (98%)
  between operations  1.29 us (2%)
    pallas_call x1, Pallas kernels, per_device(): pl.pallas_call(functools.partial(fused_kernel, side, n_rcv), out_shape=(s...  60.4 us
    pallas_call x1, Pallas kernels, per_device(): pl.pallas_call(refresh_kernel, out_shape=tuple((shape(x.shape, f32) for x...  2.14 us

profile of v3, /device:TPU:1, one launch (start us, length us, event | category | flops | bytes accessed | tf_op | source)
XLA Modules:
  0.0 63.8 jit_solution(10192186823963563179)
XLA Ops:
  1.3 60.4 %shard_map.154 = (f32[96,128]{1,0:T(8,128)}, f32[128,128]{1,0:T(8,128)}, f32[256,128]{1,0:T(8,128)}, f32[16,128]{1,0:T(8,128)}) custom-call(bf16[1,1,32,256,256]{4,3,2,1,0:T(8,128)(2,1)} %counts_hbm.1, s32[1,1,32]{2,1,0:T(1,128)} %sid_hbm.1, s32[1,1,32]{2,1,0:T(1,128)} %rid_hbm.1, s32[1,1,32]{2,1,0:T(1,128)} %aid_hbm.1, s32[1,1]{1,0:T(1,128)S(6)} %copy.17.fill_hbm, ...), custom_call_target="tpu_custom_call" | custom-call | tf_op jit(solution)/shard_map/pallas_call | solution.py:605
  61.7 2.1 %shard_map.155 = (f32[1,96,128]{2,1,0:T(8,128)}, f32[1,96,128]{2,1,0:T(8,128)}, f32[1,96,128]{2,1,0:T(8,128)}, f32[1,96,128]{2,1,0:T(8,128)}, f32[96,256]{1,0:T(8,128)}, /*index=5*/f32[96,256]{1,0:T(8,128)}) custom-call(f32[1,96,128]{2,1,0:T(8,128)} %refs_0_.1, f32[1,96,128]{2,1,0:T(8,128)} %refs_1_.1, f32[1,96,128]{2,1,0:T(8,128)} %refs_2_.1, ...), custom_call_target="tpu_custom_call" | custom-call | tf_op jit(solution)/shard_map/pallas_call | solution.py:675

commit v4 on v3

--- a/solution.py
+++ b/solution.py
@@ -111,12 +111,6 @@
 
 def settle(sem, like):
     pltpu.make_async_copy(like, like, sem).wait()
-
-
-def split3(value):
-    high = value.astype(bf16).astype(f32)
-    middle = (value - high).astype(bf16).astype(f32)
-    return high, middle, value - high - middle
 
 
 def fused_kernel(
@@ -169,6 +163,8 @@
     act_dst,
     sum_src,
     sum_dst,
+    tot_src,
+    tot_dst,
     load_sem,
     near_sems,
     ring_send,
@@ -177,6 +173,7 @@
     done_recv,
     last_sems,
     pair_sems,
+    tot_sems,
 ):
     y, z, rcv = place(side)
     half = side // 2
@@ -266,6 +263,28 @@
     settle(load_sem.at[2], ids)
     ageo_ref[...] = turned(geometric(act_ref[0], act_ref[1]))
 
+    send_row = jnp.sum(turned(jnp.exp(own_ref[2] - own_ref[3])), axis=0, keepdims=True)
+    recv_row = jnp.sum(turned(jnp.exp(own_ref[0] - own_ref[1])), axis=0, keepdims=True)
+    tot_src[0, 0:1] = send_row
+    tot_src[0, 1:2] = recv_row
+
+    def totals_in(level):
+        settle(tot_sems.at[level, 1], tot_dst.at[level, pl.ds(0, (n_rcv, side, side)[level] - 1)])
+        value = tot_dst[level, 0]
+        for index in range(1, (n_rcv, side, side)[level]):
+            value = value + tot_dst[level, index]
+        return value
+
+    def exchange_totals(level):
+        if level:
+            tot_src[level] = totals_in(level - 1)
+        me = (rcv, y, z)[level]
+        tot_dst[level, me] = tot_src[level]
+        group = Group((tot_sems.at[level, 0], tot_sems.at[level, 1]))
+        for o in range(1, (n_rcv, side, side)[level]):
+            device = peer_r(rcv, n_rcv, o) if level == 0 else to_ring(level - 1, o)
+            group.start(tot_src.at[level], tot_dst.at[level, me], device)
+
     def link(slot, carry):
         b, c = ids[0, 0, slot], ids[1, 0, slot]
         before_b, before_c = jnp.int32(slots), jnp.int32(slots)
@@ -287,9 +306,11 @@
 
         return body
 
+    exchange_totals(0)
     lax.fori_loop(0, slots, link, 0)
     for index in range(1, len(pieces)):
         forward(index)
+    exchange_totals(1)
     for index in range(len(pieces)):
         onward(index)
     for kind in (0, 1):
@@ -297,6 +318,7 @@
         for sign in (1, -1):
             ring[kind].start(part, part, to_ring(kind, sign))
 
+    exchange_totals(2)
     settle(pair_sems.at[0, 1], sgeo_ref.at[pl.ds(0, n_rcv - 1)])
 
     def scale(slot, carry):
@@ -310,15 +332,7 @@
     lax.fori_loop(0, slots, scale, 0, unroll=4)
     lax.fori_loop(0, blocks, final(1, last_recv), 0)
     lax.fori_loop(0, send_blocks, final(0, last_send), 0)
-    send_row = jnp.sum(turned(jnp.exp(own_ref[2] - own_ref[3])), axis=0, keepdims=True)
-    recv_row = jnp.sum(turned(jnp.exp(own_ref[0] - own_ref[1])), axis=0, keepdims=True)
-    row_id = lax.broadcasted_iota(jnp.int32, (16, lanes), 0)
-    totals = jnp.zeros((16, lanes), f32)
-    for index, row in enumerate(split3(send_row) + split3(recv_row)):
-        totals = jnp.where(row_id == index, row, totals)
     act_chunk = actions // n_rcv
-    for chunk in range(n_rcv):
-        act_own[chunk, act_chunk:] = totals.astype(bf16)
     send_slots[slots] = jnp.zeros(send_slots.shape[1:], f32)
     recv_slots[slots] = jnp.zeros(recv_slots.shape[1:], f32)
     settle(load_sem.at[3], fill)
@@ -329,13 +343,11 @@
 
     live_count = fill[0, 0]
 
-    def one_tile(slot):
-        c = ids[1, 0, slot]
-        live = jnp.where(slot < live_count, 1.0, 0.0).astype(f32)
-        begin = c * span
+    def recv_block(slot):
+        begin = ids[1, 0, slot] * span
         ty, tz = begin // side, lax.rem(begin, side)
         down = slot_at(ty - y, side)
-        recv = jnp.concatenate(
+        return jnp.concatenate(
             [
                 jnp.concatenate(
                     [top_ref[ty, slot_at(tz + e - z, side)] for e in range(span)], axis=1
@@ -344,20 +356,37 @@
             ],
             axis=0,
         )
-        recv_pad = jnp.concatenate([recv, jnp.zeros((lanes - rank, edge), bf16)], axis=0)
-        scaled = scaled_ref[slot]
-        expected = jnp.dot(scaled, recv_pad, preferred_element_type=f32)
-        ratios = (counts[slot].astype(f32) * live / expected).astype(bf16)
+
+    def padded(recv):
+        return jnp.concatenate([recv, jnp.zeros((lanes - rank, edge), bf16)], axis=0)
+
+    def ratio_tile(slot):
+        live = jnp.where(slot < live_count, 1.0, 0.0).astype(f32)
+        expected = jnp.dot(
+            scaled_ref[slot], padded(recv_block(slot)), preferred_element_type=f32
+        )
+        return (counts[slot].astype(f32) * live / expected).astype(bf16)
+
+    def ratio_group(group, carry):
+        done = [ratio_tile(group * unroll + u) for u in range(unroll)]
+        for u, ratios in enumerate(done):
+            counts[group * unroll + u] = ratios
+        return carry
+
+    lax.fori_loop(0, slots // unroll, ratio_group, 0)
+
+    def stat_tile(slot):
+        recv, scaled, ratios = recv_block(slot), scaled_ref[slot], counts[slot]
         toward_send = lax.dot_general(
-            ratios, recv_pad, (((1,), (1,)), ((), ())), preferred_element_type=f32
+            ratios, padded(recv), (((1,), (1,)), ((), ())), preferred_element_type=f32
         )
         toward_recv = jnp.dot(turned_ref[slot], ratios, preferred_element_type=f32)
         send_term = scaled.astype(f32) * toward_send
         recv_term = recv.astype(f32) * toward_recv
         return send_term, recv_term, jnp.sum(send_term, axis=0, keepdims=True)
 
-    def one_group(group, carry):
-        done = [one_tile(group * unroll + u) for u in range(unroll)]
+    def stat_group(group, carry):
+        done = [stat_tile(group * unroll + u) for u in range(unroll)]
         for u, (send_term, recv_term, act_term) in enumerate(done):
             slot = group * unroll + u
             send_slots[slot] = send_term + send_slots[prev[0, slot]]
@@ -365,7 +394,7 @@
             act_rows[pl.ds(slot, 1), :] = act_term
         return carry
 
-    lax.fori_loop(0, slots // unroll, one_group, 0)
+    lax.fori_loop(0, slots // unroll, stat_group, 0)
 
     action_id = lax.broadcasted_iota(jnp.int32, (actions, slots), 0)
     onehot = jnp.where(action_id == aid_row[...], 1.0, 0.0).astype(f32)
@@ -373,26 +402,29 @@
         onehot, act_rows[...], preferred_element_type=f32, precision=lax.Precision.HIGHEST
     )
     for chunk in range(n_rcv):
-        act_own[chunk, :act_chunk] = act_sum[chunk * act_chunk : (chunk + 1) * act_chunk].astype(
-            bf16
-        )
+        act_own[chunk] = act_sum[chunk * act_chunk : (chunk + 1) * act_chunk].astype(bf16)
     acts = Group((pair_sems.at[1, 0], pair_sems.at[1, 1]))
     for o in range(1, n_rcv):
         other = lax.rem(rcv + o, n_rcv)
         acts.start(act_own.at[other], act_dst.at[rcv], {"rcv": other})
     act_dst[rcv] = act_own[rcv]
 
-    def hand_over(block, carry):
-        value = recv_slots[last_recv[block]].astype(bf16)
-        begin = block * span
-        ty, tz = begin // side, lax.rem(begin, side)
-        for e in range(span):
-            columns = value[:, e * lanes : (e + 1) * lanes]
-            parts[0, ty, slot_at(tz + e - z, side)] = columns[:rows]
-            parts[1, tz + e, slot_at(ty - y, side)] = columns[rows:]
-        return carry
-
-    lax.fori_loop(0, blocks, hand_over, 0, unroll=2)
+    def hand_over(kind, distance):
+        line = block_at(kind, distance)
+        if kind == 0:
+            for block in range(side // span):
+                table = last_recv[line * (side // span) + block]
+                value = recv_slots[table, pl.ds(0, rows), :].astype(bf16)
+                for e in range(span):
+                    slot = slot_at(block * span + e - z, side)
+                    parts[0, line, slot] = value[:, e * lanes : (e + 1) * lanes]
+        else:
+            block = line // span
+            column = pl.multiple_of(lax.rem(line, span) * lanes, lanes)
+            for ty in range(side):
+                table = last_recv[ty * (side // span) + block]
+                value = recv_slots[table, pl.ds(rows, rows), pl.ds(column, lanes)]
+                parts[1, line, slot_at(ty - y, side)] = value.astype(bf16)
 
     def piece_of(kind, distance, start, size):
         return parts.at[kind, block_at(kind, distance), pl.ds(start, size)]
@@ -461,15 +493,6 @@
         for o in far_first(side):
             group.start(sum_src.at[level], sum_dst.at[level, me], to_ring(level, o))
 
-    def split_totals(value):
-        tail = value[act_chunk:]
-        result = jnp.zeros_like(tail)
-        for base in (0, 3):
-            row = tail[base : base + 1] + (tail[base + 1 : base + 2] + tail[base + 2 : base + 3])
-            for index, part in enumerate(split3(row)):
-                result = jnp.where(row_id == base + index, part, result)
-        return jnp.concatenate([value[:act_chunk], result], axis=0)
-
     last = [Group((last_sems.at[kind, 0], last_sems.at[kind, 1])) for kind in (0, 1)]
 
     def finish(index):
@@ -490,8 +513,14 @@
                         near_peer[kind](y, z, side, offset),
                     )
 
+    for distance in (half, half - 1, 1 - half):
+        for kind in (0, 1):
+            hand_over(kind, distance)
     for index in backwards:
         far_parts(index)
+    for distance in (2, -2, 1, -1, 0):
+        for kind in (0, 1):
+            hand_over(kind, distance)
 
     def give(block, carry):
         value = send_slots[last_send[block]].astype(bf16)
@@ -507,23 +536,22 @@
     send_dst[rcv] = send_part[rcv]
 
     settle(pair_sems.at[1, 1], act_dst.at[pl.ds(0, n_rcv - 1)])
-    spread(0, split_totals(total_of(act_dst, n_rcv)))
+    spread(0, total_of(act_dst, n_rcv))
     for index in backwards:
         join(index)
     settle(pair_sems.at[2, 1], sum_dst.at[0, pl.ds(0, side - 1)])
-    spread(1, split_totals(total_of(sum_dst.at[0], side)))
+    spread(1, total_of(sum_dst.at[0], side))
     for index in backwards:
         finish(index)
     for kind in (0, 1):
         near_dst[kind, 0] = near_src[kind, 0]
     settle(pair_sems.at[3, 1], sum_dst.at[1, pl.ds(0, side - 1)])
-    full = total_of(sum_dst.at[1], side)
-    act_out[pl.ds(rcv * act_chunk, act_chunk), :] = full[:act_chunk]
+    act_out[pl.ds(rcv * act_chunk, act_chunk), :] = total_of(sum_dst.at[1], side)
     own = act_out.at[pl.ds(rcv * act_chunk, act_chunk), :]
     back = Group((pair_sems.at[5, 0], pair_sems.at[5, 1]))
     for o in range(1, n_rcv):
         back.start(own, own, peer_r(rcv, n_rcv, o))
-    tot_out[...] = full[act_chunk:]
+    tot_out[...] = totals_in(2)
     settle(pair_sems.at[4, 1], send_dst.at[pl.ds(0, n_rcv - 1)])
     send_out[...] = total_of(send_dst, n_rcv)
 
@@ -531,6 +559,9 @@
         settle(near_sems.at[kind, 0], refs[kind].at[0, pl.ds(0, side - 1)])
         settle(ring_send.at[0, kind], refs[kind].at[pl.ds(0, side - 1)])
         settle(ring_send.at[1, kind], refs[kind].at[pl.ds(0, side - 1)])
+    for level in range(3):
+        like = tot_dst.at[level, pl.ds(0, (n_rcv, side, side)[level] - 1)]
+        settle(tot_sems.at[level, 0], like)
     settle(pair_sems.at[0, 0], sgeo_ref.at[pl.ds(0, n_rcv - 1)])
     settle(pair_sems.at[1, 0], act_dst.at[pl.ds(0, n_rcv - 1)])
     settle(pair_sems.at[2, 0], sum_dst.at[0, pl.ds(0, side - 1)])
@@ -559,11 +590,10 @@
     col = lax.broadcasted_iota(jnp.int32, (rank, lanes), 1)
 
     def column(index):
-        parts = [tot_ref[pl.ds(index + part, 1), :] for part in range(3)]
-        wide = jnp.broadcast_to(parts[0] + (parts[1] + parts[2]), (rank, lanes))
+        wide = jnp.broadcast_to(tot_ref[pl.ds(index, 1), :], (rank, lanes))
         return jnp.sum(jnp.where(row == col, wide, 0.0), axis=1, keepdims=True)
 
-    send_total, recv_total = column(0), column(3)
+    send_total, recv_total = column(0), column(1)
     act_total = jnp.sum(jnp.exp(as_ref[...] - ar_ref[...]), axis=1, keepdims=True)
     ss_out[0] = refresh(ss_ref[0], prior_shape + send_ref[...].T[:rank])
     sr_out[0] = refresh(sr_ref[0], prior_rate + recv_total * act_total)
@@ -600,7 +630,7 @@
     landing = pltpu.VMEM((2, 2, side, rows, lanes), bf16)
     near = pltpu.VMEM((2, side, rows, lanes), bf16)
     sender = pltpu.VMEM((n_rcv, lanes, lanes), bf16)
-    chunk = actions // n_rcv + 16
+    chunk = actions // n_rcv
 
     recv_stat, send_stat, act_stat, totals = pl.pallas_call(
         functools.partial(fused_kernel, side, n_rcv),
@@ -608,7 +638,7 @@
             shape((rank, lanes), f32),
             shape((lanes, lanes), f32),
             shape((actions, lanes), f32),
-            shape((16, lanes), f32),
+            shape((2, lanes), f32),
         ),
         in_specs=[hbm] * 11,
         out_specs=(vmem,) * 4,
@@ -645,6 +675,8 @@
             pltpu.VMEM((n_rcv, chunk, lanes), bf16),
             pltpu.VMEM((2, chunk, lanes), bf16),
             pltpu.VMEM((2, side, chunk, lanes), bf16),
+            pltpu.VMEM((3, 2, lanes), f32),
+            pltpu.VMEM((3, max(side, n_rcv), 2, lanes), f32),
             dma((6,)),
             dma((2, 3)),
             dma((2, 2)),
@@ -653,6 +685,7 @@
             dma((2, 3)),
             dma((2, 2)),
             dma((6, 2)),
+            dma((3, 2)),
         ],
         compiler_params=pltpu.CompilerParams(
             collective_id=0, has_side_effects=True, vmem_limit_bytes=whole_vmem

time: 63.9 us -> 60.6 us (0.948)
  Pallas kernels: 62.5 us -> 59.2 us
    pallas_call x1, Pallas kernels: 60.4 us -> 57 us  [per_device(): pl.pallas_call(functools.partial(fused_kernel, side, n_rcv), out_shape=(s...]
where the time goes in v4:
time: 60.6 us; the launch traced here: 60.4 us
  Pallas kernels  59.2 us (98%)
  between operations  1.29 us (2%)
    pallas_call x1, Pallas kernels, per_device(): pl.pallas_call(functools.partial(fused_kernel, side, n_rcv), out_shape=(s...  57 us
    pallas_call x1, Pallas kernels, per_device(): pl.pallas_call(refresh_kernel, out_shape=tuple((shape(x.shape, f32) for x...  2.14 us

profile of v4, /device:TPU:1, one launch (start us, length us, event | category | flops | bytes accessed | tf_op | source)
XLA Modules:
  0.0 60.4 jit_solution(14656178724523091100)
XLA Ops:
  1.3 57.0 %shard_map.154 = (f32[96,128]{1,0:T(8,128)}, f32[128,128]{1,0:T(8,128)}, f32[256,128]{1,0:T(8,128)}, f32[2,128]{1,0:T(2,128)}) custom-call(bf16[1,1,32,256,256]{4,3,2,1,0:T(8,128)(2,1)} %counts_hbm.1, s32[1,1,32]{2,1,0:T(1,128)} %sid_hbm.1, s32[1,1,32]{2,1,0:T(1,128)} %rid_hbm.1, s32[1,1,32]{2,1,0:T(1,128)} %aid_hbm.1, s32[1,1]{1,0:T(1,128)S(6)} %copy.17.fill_hbm, ...), custom_call_target="tpu_custom_call" | custom-call | tf_op jit(solution)/shard_map/pallas_call | solution.py:635
  58.3 2.1 %shard_map.155 = (f32[1,96,128]{2,1,0:T(8,128)}, f32[1,96,128]{2,1,0:T(8,128)}, f32[1,96,128]{2,1,0:T(8,128)}, f32[1,96,128]{2,1,0:T(8,128)}, f32[96,256]{1,0:T(8,128)}, /*index=5*/f32[96,256]{1,0:T(8,128)}) custom-call(f32[1,96,128]{2,1,0:T(8,128)} %refs_0_.1, f32[1,96,128]{2,1,0:T(8,128)} %refs_1_.1, f32[1,96,128]{2,1,0:T(8,128)} %refs_2_.1, ...), custom_call_target="tpu_custom_call" | custom-call | tf_op jit(solution)/shard_map/pallas_call | solution.py:708

commit v5 on v4

--- a/solution.py
+++ b/solution.py
@@ -537,20 +537,22 @@
 
     settle(pair_sems.at[1, 1], act_dst.at[pl.ds(0, n_rcv - 1)])
     spread(0, total_of(act_dst, n_rcv))
-    for index in backwards:
-        join(index)
+    join(backwards[0])
+    join(backwards[1])
     settle(pair_sems.at[2, 1], sum_dst.at[0, pl.ds(0, side - 1)])
     spread(1, total_of(sum_dst.at[0], side))
-    for index in backwards:
-        finish(index)
-    for kind in (0, 1):
-        near_dst[kind, 0] = near_src[kind, 0]
+    join(backwards[2])
+    finish(backwards[0])
+    finish(backwards[1])
     settle(pair_sems.at[3, 1], sum_dst.at[1, pl.ds(0, side - 1)])
     act_out[pl.ds(rcv * act_chunk, act_chunk), :] = total_of(sum_dst.at[1], side)
     own = act_out.at[pl.ds(rcv * act_chunk, act_chunk), :]
     back = Group((pair_sems.at[5, 0], pair_sems.at[5, 1]))
     for o in range(1, n_rcv):
         back.start(own, own, peer_r(rcv, n_rcv, o))
+    finish(backwards[2])
+    for kind in (0, 1):
+        near_dst[kind, 0] = near_src[kind, 0]
     tot_out[...] = totals_in(2)
     settle(pair_sems.at[4, 1], send_dst.at[pl.ds(0, n_rcv - 1)])
     send_out[...] = total_of(send_dst, n_rcv)

time: 60.6 us -> 59.8 us (0.987)
  Pallas kernels: 59.2 us -> 58.4 us
    pallas_call x1, Pallas kernels: 57 us -> 56.3 us  [per_device(): pl.pallas_call(functools.partial(fused_kernel, side, n_rcv), out_shape=(s...]
where the time goes in v5:
time: 59.8 us; the launch traced here: 59.7 us
  Pallas kernels  58.4 us (98%)
  between operations  1.29 us (2%)
    pallas_call x1, Pallas kernels, per_device(): pl.pallas_call(functools.partial(fused_kernel, side, n_rcv), out_shape=(s...  56.3 us
    pallas_call x1, Pallas kernels, per_device(): pl.pallas_call(refresh_kernel, out_shape=tuple((shape(x.shape, f32) for x...  2.14 us

profile of v5, /device:TPU:1, one launch (start us, length us, event | category | flops | bytes accessed | tf_op | source)
XLA Modules:
  0.0 59.7 jit_solution(16137741569654015417)
XLA Ops:
  1.3 56.3 %shard_map.154 = (f32[96,128]{1,0:T(8,128)}, f32[128,128]{1,0:T(8,128)}, f32[256,128]{1,0:T(8,128)}, f32[2,128]{1,0:T(2,128)}) custom-call(bf16[1,1,32,256,256]{4,3,2,1,0:T(8,128)(2,1)} %counts_hbm.1, s32[1,1,32]{2,1,0:T(1,128)} %sid_hbm.1, s32[1,1,32]{2,1,0:T(1,128)} %rid_hbm.1, s32[1,1,32]{2,1,0:T(1,128)} %aid_hbm.1, s32[1,1]{1,0:T(1,128)S(6)} %copy.17.fill_hbm, ...), custom_call_target="tpu_custom_call" | custom-call | tf_op jit(solution)/shard_map/pallas_call | solution.py:637
  57.5 2.1 %shard_map.155 = (f32[1,96,128]{2,1,0:T(8,128)}, f32[1,96,128]{2,1,0:T(8,128)}, f32[1,96,128]{2,1,0:T(8,128)}, f32[1,96,128]{2,1,0:T(8,128)}, f32[96,256]{1,0:T(8,128)}, /*index=5*/f32[96,256]{1,0:T(8,128)}) custom-call(f32[1,96,128]{2,1,0:T(8,128)} %refs_0_.1, f32[1,96,128]{2,1,0:T(8,128)} %refs_1_.1, f32[1,96,128]{2,1,0:T(8,128)} %refs_2_.1, ...), custom_call_target="tpu_custom_call" | custom-call | tf_op jit(solution)/shard_map/pallas_call | solution.py:710

commit v6 on v5

--- a/solution.py
+++ b/solution.py
@@ -518,9 +518,21 @@
             hand_over(kind, distance)
     for index in backwards:
         far_parts(index)
-    for distance in (2, -2, 1, -1, 0):
+    for distance in (2, -2):
         for kind in (0, 1):
             hand_over(kind, distance)
+    settle(pair_sems.at[1, 1], act_dst.at[pl.ds(0, n_rcv - 1)])
+    spread(0, total_of(act_dst, n_rcv))
+    for distance in (1, -1):
+        for kind in (0, 1):
+            hand_over(kind, distance)
+    join(backwards[0])
+    join(backwards[1])
+    settle(pair_sems.at[2, 1], sum_dst.at[0, pl.ds(0, side - 1)])
+    spread(1, total_of(sum_dst.at[0], side))
+    join(backwards[2])
+    for kind in (0, 1):
+        hand_over(kind, 0)
 
     def give(block, carry):
         value = send_slots[last_send[block]].astype(bf16)
@@ -535,13 +547,6 @@
         sends.start(send_part.at[other], send_dst.at[rcv], {"rcv": other})
     send_dst[rcv] = send_part[rcv]
 
-    settle(pair_sems.at[1, 1], act_dst.at[pl.ds(0, n_rcv - 1)])
-    spread(0, total_of(act_dst, n_rcv))
-    join(backwards[0])
-    join(backwards[1])
-    settle(pair_sems.at[2, 1], sum_dst.at[0, pl.ds(0, side - 1)])
-    spread(1, total_of(sum_dst.at[0], side))
-    join(backwards[2])
     finish(backwards[0])
     finish(backwards[1])
     settle(pair_sems.at[3, 1], sum_dst.at[1, pl.ds(0, side - 1)])

time: 59.8 us -> 59.9 us (level)
  no operation moved by 1% of the time
where the time goes in v6:
time: 59.9 us; the launch traced here: 59.8 us
  Pallas kernels  58.5 us (98%)
  between operations  1.29 us (2%)
    pallas_call x1, Pallas kernels, per_device(): pl.pallas_call(functools.partial(fused_kernel, side, n_rcv), out_shape=(s...  56.4 us
    pallas_call x1, Pallas kernels, per_device(): pl.pallas_call(refresh_kernel, out_shape=tuple((shape(x.shape, f32) for x...  2.14 us

profile of v6, /device:TPU:1, one launch (start us, length us, event | category | flops | bytes accessed | tf_op | source)
XLA Modules:
  0.0 59.8 jit_solution(15610183838950915466)
XLA Ops:
  1.3 56.4 %shard_map.154 = (f32[96,128]{1,0:T(8,128)}, f32[128,128]{1,0:T(8,128)}, f32[256,128]{1,0:T(8,128)}, f32[2,128]{1,0:T(2,128)}) custom-call(bf16[1,1,32,256,256]{4,3,2,1,0:T(8,128)(2,1)} %counts_hbm.1, s32[1,1,32]{2,1,0:T(1,128)} %sid_hbm.1, s32[1,1,32]{2,1,0:T(1,128)} %rid_hbm.1, s32[1,1,32]{2,1,0:T(1,128)} %aid_hbm.1, s32[1,1]{1,0:T(1,128)S(6)} %copy.17.fill_hbm, ...), custom_call_target="tpu_custom_call" | custom-call | tf_op jit(solution)/shard_map/pallas_call | solution.py:642
  57.6 2.1 %shard_map.155 = (f32[1,96,128]{2,1,0:T(8,128)}, f32[1,96,128]{2,1,0:T(8,128)}, f32[1,96,128]{2,1,0:T(8,128)}, f32[1,96,128]{2,1,0:T(8,128)}, f32[96,256]{1,0:T(8,128)}, /*index=5*/f32[96,256]{1,0:T(8,128)}) custom-call(f32[1,96,128]{2,1,0:T(8,128)} %refs_0_.1, f32[1,96,128]{2,1,0:T(8,128)} %refs_1_.1, f32[1,96,128]{2,1,0:T(8,128)} %refs_2_.1, ...), custom_call_target="tpu_custom_call" | custom-call | tf_op jit(solution)/shard_map/pallas_call | solution.py:715
